TPU v7x, 512 devices: a whole 4x4x16 slice. The times are simulated.
512 devices in a mesh: seq: 64 (over z, y), head: 8 (over x, core).
Axes of the slice: x: 4, y: 4, z: 16, core: 2. Of those that a mesh axis runs over, the one named last changes fastest.
Arguments:
- queries: bfloat16 [32768, 4096], P(('seq', 'head')), may hold values from -25 to 25
- key_rows: bfloat16 [32768, 4096], P(('seq', 'head')), may hold values from -6 to 6
- value_rows: bfloat16 [32768, 4096], P(('seq', 'head')), may hold values from -6 to 6
- out_grad: bfloat16 [32768, 4096], P(('seq', 'head')), may hold values from -6 to 6
- doc_ids: int32 [32768], replicated, may hold values from 0 to 15, never falling along the last dimension, each value on 1 to 4096 neighbouring positions
- picks: int32 [64, 32, 2], P('seq', 'head'), may hold values from 1 to 3, as said below
Outputs:
- attn_out: bfloat16 [32768, 4096], P(('seq', 'head'))
- query_grad: bfloat16 [32768, 4096], P(('seq', 'head'))
- key_grad: bfloat16 [32768, 4096], P(('seq', 'head'))
- value_grad: bfloat16 [32768, 4096], P(('seq', 'head'))
Inputs may be any that keep to these rules, and one draw needn't show every extreme that they name: `doc_ids`: never falling along the tokens; each document is at most 4096 tokens, one exactly that long. `picks`: for each block and head, 2 different offsets.
All inputs are finite; a program needn't handle non-finite values.
Results may differ from a plain program's by a relative error of at most 0.027.
Values may be sent and summed in bfloat16 or wider, within the bound.
No kernel may reach another device: no remote copies, remote signals or barrier semaphores. Data moves between devices by JAX's collectives and lax.ppermute only.
A program may use at most 128 MiB of HBM per device.

v0:
```python
import jax
import jax.numpy as jnp
from jax import lax
from jax.sharding import PartitionSpec as P

HEAD_DIM = 128
BLOCK = 512
REACH = 3


NEGATIVE = -1e30


def shifted(shard, axis, by):
    length = lax.axis_size(axis)
    pairs = [(i, i + by) for i in range(length) if 0 <= i + by < length]
    return lax.ppermute(shard, axis, pairs)


def block_masks(picks_block, own_index, docs_query, docs_window):
    head_count = picks_block.shape[0]
    slot_count = docs_window.shape[0]
    block_rows = docs_query.shape[0]
    chosen = jnp.concatenate(
        [own_index - picks_block, jnp.full((head_count, 1), own_index, jnp.int32)], axis=1
    )
    onehot = chosen[:, :, None] == jnp.arange(slot_count, dtype=jnp.int32)[None, None, :]
    docs_chosen = docs_window[chosen]
    key_count = chosen.shape[1]
    causal = jnp.arange(block_rows)[None, :] <= jnp.arange(block_rows)[:, None]
    earlier = jnp.arange(key_count) < key_count - 1
    allowed = jnp.logical_or(earlier[None, :, None], causal[:, None, :])
    same_doc = docs_query[None, :, None, None] == docs_chosen[:, None, :, :]
    return (onehot, jnp.logical_and(same_doc, allowed[None]))


def choose_rows(onehot, window):
    picked = jnp.einsum(
        "hkw,wbhe->hkbe", onehot.astype(jnp.bfloat16), window, preferred_element_type=jnp.float32
    )
    return picked.astype(jnp.bfloat16)


def masked_scores(query_head, keys_head, mask_head, score_scale):
    scores = (
        jnp.einsum("be,kce->bkc", query_head, keys_head, preferred_element_type=jnp.float32)
        * score_scale
    )
    return jnp.where(mask_head, scores, NEGATIVE)


def forward_heads(query_block, keys_chosen, values_chosen, allowed_mask, score_scale):

    def forward_one_head(pieces):
        query_head, keys_head, values_head, mask_head = pieces
        scores = masked_scores(query_head, keys_head, mask_head, score_scale)
        row_max = jnp.max(scores, axis=(1, 2), keepdims=True)
        row_total = jnp.sum(jnp.exp(scores - row_max), axis=(1, 2), keepdims=True)
        log_total = row_max + jnp.log(row_total)
        probs_low = jnp.exp(scores - log_total).astype(jnp.bfloat16)
        result = jnp.einsum(
            "bkc,kce->be", probs_low, values_head, preferred_element_type=jnp.float32
        ).astype(jnp.bfloat16)
        return (result, log_total[:, 0, 0])

    results, logs = lax.map(
        forward_one_head,
        (jnp.swapaxes(query_block, 0, 1), keys_chosen, values_chosen, allowed_mask),
    )
    return (jnp.swapaxes(results, 0, 1), logs)


def backward_heads(
    query_block,
    grad_block,
    out_block,
    log_block,
    keys_chosen,
    values_chosen,
    allowed_mask,
    onehot,
    score_scale,
):

    def backward_one_head(pieces):
        query_head, grad_head, out_head, log_head, keys_head, values_head, mask_head, place_head = (
            pieces
        )
        scores = masked_scores(query_head, keys_head, mask_head, score_scale)
        probs_full = jnp.exp(scores - log_head[:, None, None])
        probs_low = probs_full.astype(jnp.bfloat16)
        delta = jnp.sum(grad_head.astype(jnp.float32) * out_head.astype(jnp.float32), axis=1)
        prob_grad = jnp.einsum(
            "be,kce->bkc", grad_head, values_head, preferred_element_type=jnp.float32
        )
        score_grad = (probs_full * (prob_grad - delta[:, None, None]) * score_scale).astype(
            jnp.bfloat16
        )
        query_part = jnp.einsum(
            "bkc,kce->be", score_grad, keys_head, preferred_element_type=jnp.float32
        )
        key_part = jnp.einsum(
            "bkc,be->kce", score_grad, query_head, preferred_element_type=jnp.float32
        )
        value_part = jnp.einsum(
            "bkc,be->kce", probs_low, grad_head, preferred_element_type=jnp.float32
        )
        placing = place_head.astype(jnp.float32)
        key_slots = jnp.einsum("kw,kce->wce", placing, key_part, precision=lax.Precision.HIGHEST)
        value_slots = jnp.einsum(
            "kw,kce->wce", placing, value_part, precision=lax.Precision.HIGHEST
        )
        return (query_part, key_slots, value_slots)

    query_parts, key_slots, value_slots = lax.map(
        backward_one_head,
        (
            jnp.swapaxes(query_block, 0, 1),
            jnp.swapaxes(grad_block, 0, 1),
            jnp.swapaxes(out_block, 0, 1),
            log_block,
            keys_chosen,
            values_chosen,
            allowed_mask,
            onehot,
        ),
    )
    return (
        jnp.swapaxes(query_parts, 0, 1),
        jnp.transpose(key_slots, (1, 2, 0, 3)),
        jnp.transpose(value_slots, (1, 2, 0, 3)),
    )


def per_device(queries, key_rows, value_rows, out_grad, doc_ids, picks):
    head_total = queries.shape[1] // HEAD_DIM
    head_count = head_total // lax.axis_size("head")
    feature_width = head_count * HEAD_DIM
    row_count = queries.shape[0] * lax.axis_size("head")
    block_count = row_count // BLOCK
    shifts = (REACH + block_count - 1) // block_count
    slot_count = (shifts + 1) * block_count
    score_scale = HEAD_DIM ** (-0.5)

    def shaped(array):
        return array.reshape(-1, BLOCK, head_count, HEAD_DIM)

    query_all, key_all, value_all, grad_all = (
        lax.all_to_all(queries, "head", split_axis=1, concat_axis=0, tiled=True),
        lax.all_to_all(key_rows, "head", split_axis=1, concat_axis=0, tiled=True),
        lax.all_to_all(value_rows, "head", split_axis=1, concat_axis=0, tiled=True),
        lax.all_to_all(out_grad, "head", split_axis=1, concat_axis=0, tiled=True),
    )
    earlier_keys_list = []
    earlier_values_list = []
    for offset in range(shifts, 0, -1):
        moved_keys, moved_values = shifted((key_all, value_all), "seq", offset)
        earlier_keys_list.append(moved_keys)
        earlier_values_list.append(moved_values)
    key_window = shaped(jnp.concatenate(earlier_keys_list + [key_all], axis=0))
    value_window = shaped(jnp.concatenate(earlier_values_list + [value_all], axis=0))
    seq_index = lax.axis_index("seq")
    docs_pad = jnp.concatenate([jnp.full((shifts * row_count,), -1, jnp.int32), doc_ids])
    docs_window = lax.dynamic_slice_in_dim(
        docs_pad, seq_index * row_count, slot_count * BLOCK, 0
    ).reshape(slot_count, BLOCK)
    query_blocks = shaped(query_all)
    grad_blocks = shaped(grad_all)
    local = 0
    own_index = shifts * block_count + local
    setups = [block_masks(picks[local], own_index, docs_window[own_index], docs_window)]
    local = 0
    onehot, allowed_mask = setups[local]
    out_block, log_block = forward_heads(
        query_blocks[local],
        choose_rows(onehot, key_window),
        choose_rows(onehot, value_window),
        allowed_mask,
        score_scale,
    )
    out_blocks = [out_block]
    log_blocks = [log_block]
    attn_heads = out_blocks[0].reshape(row_count, feature_width)
    attn_out = lax.all_to_all(attn_heads, "head", split_axis=0, concat_axis=1, tiled=True)
    local = 0
    onehot, allowed_mask = setups[local]
    query_part, key_slots, value_slots = backward_heads(
        query_blocks[local],
        grad_blocks[local],
        out_blocks[local],
        log_blocks[local],
        choose_rows(onehot, key_window),
        choose_rows(onehot, value_window),
        allowed_mask,
        onehot,
        score_scale,
    )
    query_parts = query_part.astype(jnp.bfloat16)
    query_heads = query_parts.reshape(row_count, feature_width)
    key_low = key_slots.astype(jnp.bfloat16).reshape(slot_count * BLOCK, feature_width)
    value_low = value_slots.astype(jnp.bfloat16).reshape(slot_count * BLOCK, feature_width)
    key_total = key_low[shifts * row_count :].astype(jnp.float32)
    value_total = value_low[shifts * row_count :].astype(jnp.float32)
    for offset in range(1, shifts + 1):
        row_start = (shifts - offset) * row_count
        back_key, back_value = shifted(
            (
                key_low[row_start : row_start + row_count],
                value_low[row_start : row_start + row_count],
            ),
            "seq",
            -offset,
        )
        key_total = key_total + back_key.astype(jnp.float32)
        value_total = value_total + back_value.astype(jnp.float32)
    query_grad, key_grad, value_grad = (
        lax.all_to_all(query_heads, "head", split_axis=0, concat_axis=1, tiled=True),
        lax.all_to_all(
            key_total.astype(jnp.bfloat16), "head", split_axis=0, concat_axis=1, tiled=True
        ),
        lax.all_to_all(
            value_total.astype(jnp.bfloat16), "head", split_axis=0, concat_axis=1, tiled=True
        ),
    )
    return (attn_out, query_grad, key_grad, value_grad)


def solution(mesh):
    placed = (
        P(("seq", "head"), None),
        P(("seq", "head"), None),
        P(("seq", "head"), None),
        P(("seq", "head"), None),
        P(),
        P("seq", "head", None),
    )
    return jax.shard_map(
        per_device,
        mesh=mesh,
        in_specs=placed,
        out_specs=(
            P(("seq", "head"), None),
            P(("seq", "head"), None),
            P(("seq", "head"), None),
            P(("seq", "head"), None),
        ),
        check_vma=False,
    )
```

profile of v0, /device:TPU:184, one launch (start us, length us, event | category | flops | bytes accessed | tf_op | source)
XLA Modules:
  0.0 329.0 jit_solution(9482424525381147143)
XLA Ops:
  2.6 4.4 %all-to-all-start = ((bf16[64,8,512]{2,0,1:T(8,128)(2,1)}), bf16[64,8,512]{2,0,1:T(8,128)(2,1)S(1)}, u32[]{:S(2)}, u32[]{:S(2)}) async-start(bf16[64,8,512]{2,0,1:T(8,128)(2,1)} %bitcast.144), calls=%async_computation | async-start | bytes 1048576 | tf_op jit(solution)/shard_map/all_to_all | solution.py:149
  7.9 9.5 %all-to-all-done = bf16[64,8,512]{2,0,1:T(8,128)(2,1)S(1)} async-done(((bf16[64,8,512]{2,0,1:T(8,128)(2,1)}), bf16[64,8,512]{2,0,1:T(8,128)(2,1)S(1)}, u32[]{:S(2)}, u32[]{:S(2)}) %all-to-all-start) | async-done | bytes 524320 | tf_op jit(solution)/shard_map/all_to_all | solution.py:149
  23.6 7.6 %all-to-all-done.2 = bf16[64,8,512]{2,0,1:T(8,128)(2,1)S(1)} async-done(((bf16[64,8,512]{2,0,1:T(8,128)(2,1)}), bf16[64,8,512]{2,0,1:T(8,128)(2,1)S(1)}, u32[]{:S(2)}, u32[]{:S(2)}) %all-to-all-start.2) | async-done | bytes 524320 | tf_op jit(solution)/shard_map/all_to_all | solution.py:151
  39.3 4.5 %collective-permute-start.4 = (bf16[512,512]{1,0:T(8,128)(2,1)S(1)}, bf16[512,512]{1,0:T(8,128)(2,1)}, u32[]{:S(2)}, u32[]{:S(2)}) collective-permute-start(bf16[512,512]{1,0:T(8,128)(2,1)S(1)} %bitcast.204), channel_id=1, source_target_pairs={{0,16},{8,24},{16,32},{24,40},{32,48},{40,56},{48,64},{56,72},{64,... | collective-permute-start | bytes 1572872 | tf_op jit(solution)/shard_map/ppermute | solution.py:17
  47.0 4.7 %all-to-all-start.4 = ((bf16[64,8,512]{2,0,1:T(8,128)(2,1)}), bf16[64,8,512]{2,0,1:T(8,128)(2,1)S(1)}, u32[]{:S(2)}, u32[]{:S(2)}) async-start(bf16[64,8,512]{2,0,1:T(8,128)(2,1)} %bitcast.141), calls=%async_computation.4 | async-start | bytes 1048576 | tf_op jit(solution)/shard_map/all_to_all | solution.py:152
  55.4 5.3 %collective-permute-start.2 = (bf16[512,512]{1,0:T(8,128)(2,1)}, bf16[512,512]{1,0:T(8,128)(2,1)}, u32[]{:S(2)}, u32[]{:S(2)}) collective-permute-start(bf16[512,512]{1,0:T(8,128)(2,1)} %bitcast.30), channel_id=1, source_target_pairs={{0,8},{8,16},{16,24},{24,32},{32,40},{40,48},{48,56},{56,64},{64,7... | collective-permute-start | bytes 1572872 | tf_op jit(solution)/shard_map/ppermute | solution.py:17
  69.3 7.5 %collective-permute-done.4 = bf16[512,512]{1,0:T(8,128)(2,1)} collective-permute-done((bf16[512,512]{1,0:T(8,128)(2,1)S(1)}, bf16[512,512]{1,0:T(8,128)(2,1)}, u32[]{:S(2)}, u32[]{:S(2)}) %collective-permute-start.4) | collective-permute-done | bytes 524320 | tf_op jit(solution)/shard_map/ppermute | solution.py:17
  76.8 11.2 %collective-permute-done.3 = bf16[512,512]{1,0:T(8,128)(2,1)} collective-permute-done((bf16[512,512]{1,0:T(8,128)(2,1)S(1)}, bf16[512,512]{1,0:T(8,128)(2,1)}, u32[]{:S(2)}, u32[]{:S(2)}) %collective-permute-start.3) | collective-permute-done | bytes 524320 | tf_op jit(solution)/shard_map/ppermute | solution.py:17
  91.8 4.4 %fusion.50 = bf16[4,3,512,128]{3,1,2,0:T(4,128)(2,1)S(1)} fusion(bf16[4,512,4,128]{3,2,1,0:T(4,128)(2,1)} %reshape.117, s32[4,3]{1,0:T(4,128)S(1)} %concatenate.13.clone), kind=kOutput, calls=%fused_computation.67 | convolution fusion | flops 7077936 | bytes 3670064 | tf_op jit(solution)/shard_map/hkw,wbhe->hkbe/dot_general | solution.py:38
  97.7 7.2 %collective-permute-done.2 = bf16[512,512]{1,0:T(8,128)(2,1)} collective-permute-done((bf16[512,512]{1,0:T(8,128)(2,1)}, bf16[512,512]{1,0:T(8,128)(2,1)}, u32[]{:S(2)}, u32[]{:S(2)}) %collective-permute-start.2) | collective-permute-done | bytes 524320 | tf_op jit(solution)/shard_map/ppermute | solution.py:17
  104.9 12.7 %collective-permute-done.1 = bf16[512,512]{1,0:T(8,128)(2,1)} collective-permute-done((bf16[512,512]{1,0:T(8,128)(2,1)}, bf16[512,512]{1,0:T(8,128)(2,1)}, u32[]{:S(2)}, u32[]{:S(2)}) %collective-permute-start.1) | collective-permute-done | bytes 524320 | tf_op jit(solution)/shard_map/ppermute | solution.py:17
  117.6 10.7 %collective-permute-done = bf16[512,512]{1,0:T(8,128)(2,1)} collective-permute-done((bf16[512,512]{1,0:T(8,128)(2,1)}, bf16[512,512]{1,0:T(8,128)(2,1)}, u32[]{:S(2)}, u32[]{:S(2)}) %collective-permute-start) | collective-permute-done | bytes 524320 | tf_op jit(solution)/shard_map/ppermute | solution.py:17
  132.0 4.4 %fusion.47 = bf16[4,3,512,128]{3,1,2,0:T(4,128)(2,1)S(1)} fusion(bf16[4,512,4,128]{3,2,1,0:T(4,128)(2,1)} %reshape.116, s32[4,3]{1,0:T(4,128)S(1)} %concatenate.13.clone), kind=kOutput, calls=%fused_computation.66 | convolution fusion | flops 7077936 | bytes 3670064 | tf_op jit(solution)/shard_map/hkw,wbhe->hkbe/dot_general | solution.py:38
  138.0 26.6 %while.26 = (s32[]{:T(128)}, bf16[4,512,128]{2,1,0:T(8,128)(2,1)}, f32[4,512]{1,0:T(4,128)S(1)}, pred[4,512,3,512]{3,1,2,0:T(32,128)(4,1)}, bf16[4,512,128]{2,1,...) while((s32[]{:T(128)}, bf16[4,512,128]{2,1,0:T(8,128)(2,1)}, ...), condition=%wide.region_3.4_spmd, body=%wide.region_0.3_spmd.sunk | while | flops 408223232 | bytes 14438509 | solution.py:66
  164.6 54.7 %while.27 = (s32[]{:T(128)}, bf16[4,512,128]{2,1,0:T(8,128)(2,1)}, bf16[4,4,512,128]{2,3,0,1:T(8,128)(2,1)}, bf16[4,4,512,128]{2,3,0,1:T(8,128)(2,1)}, pred[4,51...) while((s32[]{:T(128)}, bf16[4,512,128]{2,1,0:T(8,128)(2,1)}, ...), condition=%wide.region_6.7_spmd, body=%wide.region_4.6_spmd.sunk | while | flops 1032060416 | bytes 29768408 | solution.py:115
  229.7 5.2 %collective-permute-start.10 = (bf16[512,512]{0,1:T(8,128)(2,1)}, bf16[512,512]{0,1:T(8,128)(2,1)}, u32[]{:S(2)}, u32[]{:S(2)}) collective-permute-start(bf16[512,512]{0,1:T(8,128)(2,1)} %bitcast.52), channel_id=1, source_target_pairs={{16,0},{24,8},{32,16},{40,24},{48,32},{56,40},{64,48},{72,56},{80,... | collective-permute-start | bytes 1572872 | tf_op jit(solution)/shard_map/ppermute | solution.py:17
  239.3 4.8 %all-to-all-start.3 = ((bf16[8,64,512]{2,1,0:T(8,128)(2,1)}), bf16[8,64,512]{2,1,0:T(8,128)(2,1)S(1)}, u32[]{:S(2)}, u32[]{:S(2)}) async-start(bf16[8,64,512]{2,1,0:T(8,128)(2,1)} %all_to_all.119), calls=%async_computation.3 | async-start | bytes 1048576 | tf_op jit(solution)/shard_map/all_to_all | solution.py:184
  245.5 5.0 %collective-permute-start.8 = (bf16[512,512]{0,1:T(8,128)(2,1)}, bf16[512,512]{0,1:T(8,128)(2,1)S(1)}, u32[]{:S(2)}, u32[]{:S(2)}) collective-permute-start(bf16[512,512]{0,1:T(8,128)(2,1)} %bitcast.46), channel_id=1, source_target_pairs={{24,0},{32,8},{40,16},{48,24},{56,32},{64,40},{72,48},{80,56},{88,... | collective-permute-start | bytes 1572872 | tf_op jit(solution)/shard_map/ppermute | solution.py:17
  252.5 6.2 %collective-permute-start.6 = (bf16[512,512]{0,1:T(8,128)(2,1)}, bf16[512,512]{0,1:T(8,128)(2,1)}, u32[]{:S(2)}, u32[]{:S(2)}) collective-permute-start(bf16[512,512]{0,1:T(8,128)(2,1)} %bitcast.44), channel_id=1, source_target_pairs={{8,0},{16,8},{24,16},{32,24},{40,32},{48,40},{56,48},{64,56},{72,6... | collective-permute-start | bytes 1572872 | tf_op jit(solution)/shard_map/ppermute | solution.py:17
  258.7 15.5 %collective-permute-done.10 = bf16[512,512]{0,1:T(8,128)(2,1)} collective-permute-done((bf16[512,512]{0,1:T(8,128)(2,1)}, bf16[512,512]{0,1:T(8,128)(2,1)}, u32[]{:S(2)}, u32[]{:S(2)}) %collective-permute-start.10) | collective-permute-done | bytes 524320 | tf_op jit(solution)/shard_map/ppermute | solution.py:17
  280.7 4.4 %all-to-all-start.7 = ((bf16[8,64,512]{2,1,0:T(8,128)(2,1)}), bf16[8,64,512]{2,1,0:T(8,128)(2,1)S(1)}, u32[]{:S(2)}, u32[]{:S(2)}) async-start(bf16[8,64,512]{2,1,0:T(8,128)(2,1)} %bitcast.54), calls=%async_computation.7 | async-start | bytes 1048576 | tf_op jit(solution)/shard_map/all_to_all | solution.py:221
  285.1 9.5 %collective-permute-done.7 = bf16[512,512]{0,1:T(8,128)(2,1)} collective-permute-done((bf16[512,512]{0,1:T(8,128)(2,1)}, bf16[512,512]{0,1:T(8,128)(2,1)}, u32[]{:S(2)}, u32[]{:S(2)}) %collective-permute-start.7) | collective-permute-done | bytes 524320 | tf_op jit(solution)/shard_map/ppermute | solution.py:17
  294.6 16.7 %collective-permute-done.6 = bf16[512,512]{0,1:T(8,128)(2,1)} collective-permute-done((bf16[512,512]{0,1:T(8,128)(2,1)}, bf16[512,512]{0,1:T(8,128)(2,1)}, u32[]{:S(2)}, u32[]{:S(2)}) %collective-permute-start.6) | collective-permute-done | bytes 524320 | tf_op jit(solution)/shard_map/ppermute | solution.py:17
  320.3 7.8 %all-to-all-done.6 = bf16[8,64,512]{2,1,0:T(8,128)(2,1)S(1)} async-done(((bf16[8,64,512]{2,1,0:T(8,128)(2,1)}), bf16[8,64,512]{2,1,0:T(8,128)(2,1)S(1)}, u32[]{:S(2)}, u32[]{:S(2)}) %all-to-all-start.6) | async-done | bytes 524320 | tf_op jit(solution)/shard_map/all_to_all | solution.py:218
  (184 shorter events, 158.1 us)
Async XLA Ops:
  0.7 20.5 %copy-start.10 = (s32[32768]{0:T(1024)S(1)}, s32[32768]{0:T(1024)}, u32[]{:S(2)}) copy-start(s32[32768]{0:T(1024)} %param.14) | copy-start | bytes 393220
  2.6 14.8 %all-to-all-start = ((bf16[64,8,512]{2,0,1:T(8,128)(2,1)}), bf16[64,8,512]{2,0,1:T(8,128)(2,1)S(1)}, u32[]{:S(2)}, u32[]{:S(2)}) async-start(bf16[64,8,512]{2,0,1:T(8,128)(2,1)} %bitcast.144), calls=%async_computation | async-start | bytes 1048576 | tf_op jit(solution)/shard_map/all_to_all | solution.py:149
  17.4 13.8 %all-to-all-start.2 = ((bf16[64,8,512]{2,0,1:T(8,128)(2,1)}), bf16[64,8,512]{2,0,1:T(8,128)(2,1)S(1)}, u32[]{:S(2)}, u32[]{:S(2)}) async-start(bf16[64,8,512]{2,0,1:T(8,128)(2,1)} %bitcast.142), calls=%async_computation.2 | async-start | bytes 1048576 | tf_op jit(solution)/shard_map/all_to_all | solution.py:151
  31.2 24.1 %copy-start.6 = (bf16[64,8,512]{2,0,1:T(8,128)(2,1)}, bf16[64,8,512]{2,0,1:T(8,128)(2,1)S(1)}, u32[]{:S(2)}) copy-start(bf16[64,8,512]{2,0,1:T(8,128)(2,1)S(1)} %all-to-all-done.2) | copy-start | bytes 1572868
  31.2 15.8 %all-to-all-start.1 = ((bf16[64,8,512]{2,0,1:T(8,128)(2,1)}), bf16[64,8,512]{2,0,1:T(8,128)(2,1)}, u32[]{:S(2)}, u32[]{:S(2)}) async-start(bf16[64,8,512]{2,0,1:T(8,128)(2,1)} %bitcast.143), calls=%async_computation.1 | async-start | bytes 1048576 | tf_op jit(solution)/shard_map/all_to_all | solution.py:150
  35.8 29.5 %collective-permute-start.5 = (bf16[512,512]{1,0:T(8,128)(2,1)S(1)}, bf16[512,512]{1,0:T(8,128)(2,1)S(1)}, u32[]{:S(2)}, u32[]{:S(2)}) collective-permute-start(bf16[512,512]{1,0:T(8,128)(2,1)S(1)} %bitcast.203), channel_id=1, source_target_pairs={{0,8},{8,16},{16,24},{24,32},{32,40},{40,48},{48,56},{56,64},{64,7... | collective-permute-start | bytes 1572872 | tf_op jit(solution)/shard_map/ppermute | solution.py:17
  39.3 37.5 %collective-permute-start.4 = (bf16[512,512]{1,0:T(8,128)(2,1)S(1)}, bf16[512,512]{1,0:T(8,128)(2,1)}, u32[]{:S(2)}, u32[]{:S(2)}) collective-permute-start(bf16[512,512]{1,0:T(8,128)(2,1)S(1)} %bitcast.204), channel_id=1, source_target_pairs={{0,16},{8,24},{16,32},{24,40},{32,48},{40,56},{48,64},{56,72},{64,... | collective-permute-start | bytes 1572872 | tf_op jit(solution)/shard_map/ppermute | solution.py:17
  43.8 44.2 %collective-permute-start.3 = (bf16[512,512]{1,0:T(8,128)(2,1)S(1)}, bf16[512,512]{1,0:T(8,128)(2,1)}, u32[]{:S(2)}, u32[]{:S(2)}) collective-permute-start(bf16[512,512]{1,0:T(8,128)(2,1)S(1)} %bitcast.205), channel_id=1, source_target_pairs={{0,24},{8,32},{16,40},{24,48},{32,56},{40,64},{48,72},{56,80},{64,... | collective-permute-start | bytes 1572872 | tf_op jit(solution)/shard_map/ppermute | solution.py:17
  47.0 18.2 %all-to-all-start.4 = ((bf16[64,8,512]{2,0,1:T(8,128)(2,1)}), bf16[64,8,512]{2,0,1:T(8,128)(2,1)S(1)}, u32[]{:S(2)}, u32[]{:S(2)}) async-start(bf16[64,8,512]{2,0,1:T(8,128)(2,1)} %bitcast.141), calls=%async_computation.4 | async-start | bytes 1048576 | tf_op jit(solution)/shard_map/all_to_all | solution.py:152
  55.4 49.5 %collective-permute-start.2 = (bf16[512,512]{1,0:T(8,128)(2,1)}, bf16[512,512]{1,0:T(8,128)(2,1)}, u32[]{:S(2)}, u32[]{:S(2)}) collective-permute-start(bf16[512,512]{1,0:T(8,128)(2,1)} %bitcast.30), channel_id=1, source_target_pairs={{0,8},{8,16},{16,24},{24,32},{32,40},{40,48},{48,56},{56,64},{64,7... | collective-permute-start | bytes 1572872 | tf_op jit(solution)/shard_map/ppermute | solution.py:17
  60.7 56.9 %collective-permute-start.1 = (bf16[512,512]{1,0:T(8,128)(2,1)}, bf16[512,512]{1,0:T(8,128)(2,1)}, u32[]{:S(2)}, u32[]{:S(2)}) collective-permute-start(bf16[512,512]{1,0:T(8,128)(2,1)} %bitcast.30), channel_id=1, source_target_pairs={{0,16},{8,24},{16,32},{24,40},{32,48},{40,56},{48,64},{56,72},{64,... | collective-permute-start | bytes 1572872 | tf_op jit(solution)/shard_map/ppermute | solution.py:17
  65.4 62.9 %collective-permute-start = (bf16[512,512]{1,0:T(8,128)(2,1)}, bf16[512,512]{1,0:T(8,128)(2,1)}, u32[]{:S(2)}, u32[]{:S(2)}) collective-permute-start(bf16[512,512]{1,0:T(8,128)(2,1)} %bitcast.30), channel_id=1, source_target_pairs={{0,24},{8,32},{16,40},{24,48},{32,56},{40,64},{48,72},{56,80},{64,... | collective-permute-start | bytes 1572872 | tf_op jit(solution)/shard_map/ppermute | solution.py:17
  221.9 17.3 %all-to-all-start.5 = ((bf16[8,64,512]{2,1,0:T(8,128)(2,1)}), bf16[8,64,512]{2,1,0:T(8,128)(2,1)S(1)}, u32[]{:S(2)}, u32[]{:S(2)}) async-start(bf16[8,64,512]{2,1,0:T(8,128)(2,1)} %all_to_all.126), calls=%async_computation.5 | async-start | bytes 1048576 | tf_op jit(solution)/shard_map/all_to_all | solution.py:217
  227.6 24.8 %collective-permute-start.11 = (bf16[512,512]{0,1:T(8,128)(2,1)}, bf16[512,512]{0,1:T(8,128)(2,1)}, u32[]{:S(2)}, u32[]{:S(2)}) collective-permute-start(bf16[512,512]{0,1:T(8,128)(2,1)} %bitcast.53), channel_id=1, source_target_pairs={{24,0},{32,8},{40,16},{48,24},{56,32},{64,40},{72,48},{80,56},{88,... | collective-permute-start | bytes 1572872 | tf_op jit(solution)/shard_map/ppermute | solution.py:17
  229.7 44.4 %collective-permute-start.10 = (bf16[512,512]{0,1:T(8,128)(2,1)}, bf16[512,512]{0,1:T(8,128)(2,1)}, u32[]{:S(2)}, u32[]{:S(2)}) collective-permute-start(bf16[512,512]{0,1:T(8,128)(2,1)} %bitcast.52), channel_id=1, source_target_pairs={{16,0},{24,8},{32,16},{40,24},{48,32},{56,40},{64,48},{72,56},{80,... | collective-permute-start | bytes 1572872 | tf_op jit(solution)/shard_map/ppermute | solution.py:17
  234.9 43.1 %collective-permute-start.9 = (bf16[512,512]{0,1:T(8,128)(2,1)}, bf16[512,512]{0,1:T(8,128)(2,1)}, u32[]{:S(2)}, u32[]{:S(2)}) collective-permute-start(bf16[512,512]{0,1:T(8,128)(2,1)} %bitcast.51), channel_id=1, source_target_pairs={{8,0},{16,8},{24,16},{32,24},{40,32},{48,40},{56,48},{64,56},{72,6... | collective-permute-start | bytes 1572872 | tf_op jit(solution)/shard_map/ppermute | solution.py:17
  239.3 41.4 %all-to-all-start.3 = ((bf16[8,64,512]{2,1,0:T(8,128)(2,1)}), bf16[8,64,512]{2,1,0:T(8,128)(2,1)S(1)}, u32[]{:S(2)}, u32[]{:S(2)}) async-start(bf16[8,64,512]{2,1,0:T(8,128)(2,1)} %all_to_all.119), calls=%async_computation.3 | async-start | bytes 1048576 | tf_op jit(solution)/shard_map/all_to_all | solution.py:184
  244.1 33.9 %copy-start.4 = (bf16[1,512,4,128]{1,3,2,0:T(8,128)(2,1)S(1)}, bf16[1,512,4,128]{1,3,2,0:T(8,128)(2,1)}, u32[]{:S(2)}) copy-start(bf16[1,512,4,128]{1,3,2,0:T(8,128)(2,1)} %get-tuple-element.229) | copy-start | bytes 1572868
  245.5 39.7 %collective-permute-start.8 = (bf16[512,512]{0,1:T(8,128)(2,1)}, bf16[512,512]{0,1:T(8,128)(2,1)S(1)}, u32[]{:S(2)}, u32[]{:S(2)}) collective-permute-start(bf16[512,512]{0,1:T(8,128)(2,1)} %bitcast.46), channel_id=1, source_target_pairs={{24,0},{32,8},{40,16},{48,24},{56,32},{64,40},{72,48},{80,56},{88,... | collective-permute-start | bytes 1572872 | tf_op jit(solution)/shard_map/ppermute | solution.py:17
  250.5 44.1 %collective-permute-start.7 = (bf16[512,512]{0,1:T(8,128)(2,1)}, bf16[512,512]{0,1:T(8,128)(2,1)}, u32[]{:S(2)}, u32[]{:S(2)}) collective-permute-start(bf16[512,512]{0,1:T(8,128)(2,1)} %bitcast.45), channel_id=1, source_target_pairs={{16,0},{24,8},{32,16},{40,24},{48,32},{56,40},{64,48},{72,56},{80,... | collective-permute-start | bytes 1572872 | tf_op jit(solution)/shard_map/ppermute | solution.py:17
  252.5 58.8 %collective-permute-start.6 = (bf16[512,512]{0,1:T(8,128)(2,1)}, bf16[512,512]{0,1:T(8,128)(2,1)}, u32[]{:S(2)}, u32[]{:S(2)}) collective-permute-start(bf16[512,512]{0,1:T(8,128)(2,1)} %bitcast.44), channel_id=1, source_target_pairs={{8,0},{16,8},{24,16},{32,24},{40,32},{48,40},{56,48},{64,56},{72,6... | collective-permute-start | bytes 1572872 | tf_op jit(solution)/shard_map/ppermute | solution.py:17
  278.0 33.3 %copy-start.5 = (bf16[1,512,4,128]{1,3,2,0:T(8,128)(2,1)S(1)}, bf16[1,512,4,128]{1,3,2,0:T(8,128)(2,1)}, u32[]{:S(2)}) copy-start(bf16[1,512,4,128]{1,3,2,0:T(8,128)(2,1)} %get-tuple-element.233) | copy-start | bytes 1572868
  280.7 33.1 %all-to-all-start.7 = ((bf16[8,64,512]{2,1,0:T(8,128)(2,1)}), bf16[8,64,512]{2,1,0:T(8,128)(2,1)S(1)}, u32[]{:S(2)}, u32[]{:S(2)}) async-start(bf16[8,64,512]{2,1,0:T(8,128)(2,1)} %bitcast.54), calls=%async_computation.7 | async-start | bytes 1048576 | tf_op jit(solution)/shard_map/all_to_all | solution.py:221
  313.8 14.4 %all-to-all-start.6 = ((bf16[8,64,512]{2,1,0:T(8,128)(2,1)}), bf16[8,64,512]{2,1,0:T(8,128)(2,1)S(1)}, u32[]{:S(2)}, u32[]{:S(2)}) async-start(bf16[8,64,512]{2,1,0:T(8,128)(2,1)} %bitcast.47), calls=%async_computation.6 | async-start | bytes 1048576 | tf_op jit(solution)/shard_map/all_to_all | solution.py:218
  (15 other events, 119.1 us)
where the time goes:
time: 331 us; the launch traced here: 329 us
  waiting for transfers between devices  120 us (36%)
  starting transfers between devices  81.2 us (25%)
  matrix products  67.2 us (20%)
  local copies, waits for them, and re-layouts  42 us (13%)
  other arithmetic  17.4 us (5%)
    ppermute x12, waiting for transfers between devices, shifted(): return lax.ppermute(shard, axis, pairs)  94.8 us
    ppermute x12, starting transfers between devices, shifted(): return lax.ppermute(shard, axis, pairs)  46.8 us
    dot_general x8, matrix products, masked_scores(): jnp.einsum('be,kce->bkc', query_head, keys_head, preferred_element_type=j...  15.5 us
    all_to_all x1, waiting for transfers between devices, per_device(): lax.all_to_all(queries, 'head', split_axis=1, concat_axis=0, tiled=True)  9.49 us
    dot_general x4, matrix products, forward_one_head(): jnp.einsum('bkc,kce->be', probs_low, values_head, preferred_element_type=...  9.24 us
    dot_general x4, matrix products, backward_one_head(): jnp.einsum('bkc,kce->be', score_grad, keys_head, preferred_element_type=j...  9.15 us
    dot_general x2, matrix products, choose_rows(): jnp.einsum('hkw,wbhe->hkbe', onehot.astype(jnp.bfloat16), window, preferr...  8.79 us
    dynamic_slice x8, local copies, waits for them, and re-layouts, forward_heads(): lax.map(forward_one_head, (jnp.swapaxes(query_block, 0, 1), keys_chosen,...  8.31 us
  transfers between devices with their start and end apart: 20, of which 12 were waited for; matrix products, arithmetic and copies ran while one was open for 9% of the time, Pallas kernels for 0%

commit v1 on v0

v1 whole, which is shorter than its diff:
```python
import functools
import math

import jax
import jax.numpy as jnp
from jax import lax
from jax.experimental import pallas as pl
from jax.experimental.pallas import tpu as pltpu
from jax.sharding import Mesh
from jax.sharding import PartitionSpec as P

HEADS = 32
HEAD_DIM = 128
BLOCK = 512
REACH = 3
GROUP = 4
DOCS = 16
WINDOW = GROUP + REACH
CHUNK = 64
PER_BLOCK = BLOCK // CHUNK
NEGATIVE = -1e30
SCALE = HEAD_DIM ** (-0.5)
SCALE_LOG2 = SCALE * math.log2(math.e)

NT = (((1,), (1,)), ((), ()))
NN = (((1,), (0,)), ((), ()))


def dot(a, b, dims=NN):
    return lax.dot_general(a, b, dims, preferred_element_type=jnp.float32)


def attend(
    picks, docs, kv, halo, qd, od, dkv, back, keys, values, keys_t, values_t, key_sum, value_sum
):
    bf16 = jnp.bfloat16
    docs_t = jnp.transpose(docs[...])
    lane = lax.broadcasted_iota(jnp.int32, (128, 128), 1).astype(jnp.float32)

    def marks(row):
        return jnp.broadcast_to(docs_t[:, row : row + 1], (128, 128)) == lane

    for b in range(WINDOW):
        rows = pl.ds(b * BLOCK, BLOCK)
        source, at = (halo, b) if b < REACH else (kv, b - REACH)
        at = pl.ds(at * PER_BLOCK, PER_BLOCK)
        key = source[at, 0].reshape(BLOCK, HEAD_DIM)
        value = source[at, 1].reshape(BLOCK, HEAD_DIM)
        keys[rows, :HEAD_DIM] = key
        values[rows, :] = value
        keys_t[b] = jnp.transpose(key)
        values_t[b, :HEAD_DIM] = jnp.transpose(value)
        values_t[b, HEAD_DIM:] = jnp.ones((16, BLOCK), bf16)
        for part in range(4):
            row = b * 4 + part
            keys[pl.ds(row * 128, 128), HEAD_DIM:] = jnp.where(marks(row), 1.0, 0.0).astype(bf16)
    key_sum[...] = jnp.zeros_like(key_sum)
    value_sum[...] = jnp.zeros_like(value_sum)

    causal = lax.broadcasted_iota(jnp.int32, (BLOCK, BLOCK), 0) <= lax.broadcasted_iota(
        jnp.int32, (BLOCK, BLOCK), 1
    )
    for j in range(GROUP):
        own = REACH + j
        at = pl.ds(j * PER_BLOCK, PER_BLOCK)
        query = qd[at, 0].reshape(BLOCK, HEAD_DIM)
        grad = qd[at, 1].reshape(BLOCK, HEAD_DIM)
        bias = [
            jnp.where(jnp.logical_or(marks(own * 4 + part), lane > DOCS), 0.0, NEGATIVE)
            for part in range(4)
        ]
        query_wide = jnp.concatenate([query, jnp.concatenate(bias, axis=0).astype(bf16)], axis=1)
        slots = [own - picks[2 * j], own - picks[2 * j + 1], own]
        rows = [pl.ds(pl.multiple_of(s * BLOCK, BLOCK), BLOCK) for s in slots]
        scores = [dot(keys[r, :], query_wide, NT) for r in rows]
        scores[2] = jnp.where(causal, scores[2], NEGATIVE)
        top = functools.reduce(
            jnp.maximum, [jnp.max(s, axis=0, keepdims=True) for s in scores]
        )
        top = top * SCALE_LOG2
        probs = [jnp.exp2(s * SCALE_LOG2 - top).astype(bf16) for s in scores]
        result = sum(dot(values_t[s], p) for s, p in zip(slots, probs))
        inverse = 1.0 / result[HEAD_DIM : HEAD_DIM + 1]
        out_t = result[:HEAD_DIM] * inverse
        od[at, 0] = jnp.transpose(out_t).astype(bf16).reshape(PER_BLOCK, CHUNK, HEAD_DIM)
        grad_full = grad.astype(jnp.float32)
        delta = jnp.sum(jnp.transpose(grad_full) * out_t, axis=0, keepdims=True)
        inverse_rows = jnp.transpose(jnp.broadcast_to(inverse, (HEAD_DIM, BLOCK)))
        grad_low = (grad_full * inverse_rows).astype(bf16)
        query_low = (query.astype(jnp.float32) * (inverse_rows * SCALE)).astype(bf16)
        query_sum = None
        for s, r, p in zip(slots, rows, probs):
            prob_grad = dot(values[r, :], grad, NT)
            score_grad = (p.astype(jnp.float32) * (prob_grad - delta)).astype(bf16)
            part = dot(keys_t[s], score_grad)
            query_sum = part if query_sum is None else query_sum + part
            key_sum[r, :] += dot(score_grad, query_low)
            value_sum[r, :] += dot(p, grad_low)
        query_sum = query_sum * (inverse * SCALE)
        od[at, 1] = jnp.transpose(query_sum).astype(bf16).reshape(PER_BLOCK, CHUNK, HEAD_DIM)

    split = REACH * BLOCK
    for target, begin, rows in ((back, 0, split), (dkv, split, GROUP * BLOCK)):
        shape = (rows // CHUNK, CHUNK, HEAD_DIM)
        target[:, 0] = key_sum[begin : begin + rows].astype(bf16).reshape(shape)
        target[:, 1] = value_sum[begin : begin + rows].astype(bf16).reshape(shape)


def attention(picks, docs, kv, halo, qd):
    low = jnp.bfloat16
    pairs = 3 * GROUP * BLOCK * BLOCK
    vmem = pl.BlockSpec(memory_space=pltpu.VMEM)
    return pl.pallas_call(
        attend,
        out_shape=(
            jax.ShapeDtypeStruct(qd.shape, low),
            jax.ShapeDtypeStruct(kv.shape, low),
            jax.ShapeDtypeStruct(halo.shape, low),
        ),
        in_specs=[pl.BlockSpec(memory_space=pltpu.SMEM)] + [vmem] * 4,
        out_specs=(vmem,) * 3,
        scratch_shapes=[
            pltpu.VMEM((WINDOW * BLOCK, 2 * HEAD_DIM), low),
            pltpu.VMEM((WINDOW * BLOCK, HEAD_DIM), low),
            pltpu.VMEM((WINDOW, HEAD_DIM, BLOCK), low),
            pltpu.VMEM((WINDOW, HEAD_DIM + 16, BLOCK), low),
            pltpu.VMEM((WINDOW * BLOCK, HEAD_DIM), jnp.float32),
            pltpu.VMEM((WINDOW * BLOCK, HEAD_DIM), jnp.float32),
        ],
        compiler_params=pltpu.CompilerParams(vmem_limit_bytes=56 * 1024 * 1024),
        cost_estimate=pl.CostEstimate(
            flops=12 * pairs * HEAD_DIM,
            bytes_accessed=6 * 1024 * 1024,
            transcendentals=pairs,
        ),
        name="attend",
    )(picks, docs, kv, halo, qd)


def per_device(queries, key_rows, value_rows, out_grad, doc_ids, picks):
    plane = lax.axis_index("z")
    forward = [(i, i + 1) for i in range(lax.axis_size("z") - 1)]
    backward = [(i + 1, i) for i in range(lax.axis_size("z") - 1)]

    def to_heads(first, second):
        both = jnp.stack([first, second]).reshape(2, CHUNK, PER_BLOCK, GROUP, HEAD_DIM)
        both = jnp.transpose(both, (3, 2, 0, 1, 4)).reshape(HEADS, 2, CHUNK, HEAD_DIM)
        return lax.all_to_all(both, ("y", "h"), split_axis=0, concat_axis=0)

    def to_rows(both):
        both = lax.all_to_all(both, ("y", "h"), split_axis=0, concat_axis=0)
        both = both.reshape(GROUP, PER_BLOCK, 2, CHUNK, HEAD_DIM)
        both = jnp.transpose(both, (2, 3, 1, 0, 4)).reshape(2, CHUNK, HEADS * HEAD_DIM)
        return both[0], both[1]

    kv = to_heads(key_rows, value_rows)
    halo = lax.ppermute(kv[PER_BLOCK:], "z", forward)
    qd = to_heads(queries, out_grad)

    picks_plane = lax.all_gather(picks, "y", axis=0, tiled=True)
    picks_here = lax.dynamic_index_in_dim(picks_plane, lax.axis_index("y"), 1, False).reshape(-1)
    docs_pad = jnp.concatenate([jnp.full((REACH * BLOCK,), DOCS, jnp.int32), doc_ids])
    docs = lax.dynamic_slice_in_dim(docs_pad, plane * (GROUP * BLOCK), WINDOW * BLOCK, 0)
    docs = jnp.pad(docs.astype(jnp.float32).reshape(WINDOW * 4, 128), ((0, 4), (0, 0)))

    od, dkv, back = attention(picks_here, docs, kv, halo, qd)
    back = lax.ppermute(back, "z", backward)
    attn_out, query_grad = to_rows(od)
    back = jnp.pad(back, ((PER_BLOCK, 0), (0, 0), (0, 0), (0, 0)))
    dkv = (dkv.astype(jnp.float32) + back.astype(jnp.float32)).astype(jnp.bfloat16)
    key_grad, value_grad = to_rows(dkv)
    return attn_out, query_grad, key_grad, value_grad


def solution(mesh):
    planes = mesh.shape["seq"] // GROUP
    parts = Mesh(mesh.devices.reshape(planes, GROUP, mesh.shape["head"]), ("z", "y", "h"))
    rows = P(("z", "y", "h"), None)
    return jax.shard_map(
        per_device,
        mesh=parts,
        in_specs=(rows, rows, rows, rows, P(), P(("z", "y"), "h", None)),
        out_specs=(rows,) * 4,
        check_vma=False,
    )
```

time: 331 us -> 127 us (0.38)
  the two profiles are of different devices: /device:TPU:184 before, /device:TPU:289 now
where the time goes in v1:
time: 127 us; the launch traced here: 126 us
  waiting for transfers between devices  52.1 us (41%)
  starting transfers between devices  31.1 us (24%)
  Pallas kernels  17.3 us (14%)
  local copies, waits for them, and re-layouts  12.8 us (10%)
  blocking collectives  8.68 us (7%)
  other arithmetic  3.57 us (3%)
    all_to_all x2, waiting for transfers between devices, to_rows(): both = lax.all_to_all(both, ('y', 'h'), split_axis=0, concat_axis=0)  22.5 us
    all_to_all x2, waiting for transfers between devices, to_heads(): return lax.all_to_all(both, ('y', 'h'), split_axis=0, concat_axis=0)  18.8 us
    pallas_call x1, Pallas kernels, attention(): pl.pallas_call(attend, out_shape=(jax.ShapeDtypeStruct(qd.shape, low), ja...  17.3 us
    all_to_all x2, starting transfers between devices, to_rows(): both = lax.all_to_all(both, ('y', 'h'), split_axis=0, concat_axis=0)  12.7 us
    all_to_all x2, starting transfers between devices, to_heads(): return lax.all_to_all(both, ('y', 'h'), split_axis=0, concat_axis=0)  11.9 us
    all_gather x1, blocking collectives, per_device(): picks_plane = lax.all_gather(picks, 'y', axis=0, tiled=True)  8.68 us
    ppermute x1, waiting for transfers between devices, per_device(): back = lax.ppermute(back, 'z', backward)  7.35 us
    squeeze x4, local copies, waits for them, and re-layouts, to_rows(): return (both[0], both[1])  4.73 us
  transfers between devices with their start and end apart: 6, of which 6 were waited for; matrix products, arithmetic and copies ran while one was open for 7% of the time, Pallas kernels for 0%

profile of v1, /device:TPU:289, one launch (start us, length us, event | category | flops | bytes accessed | tf_op | source)
XLA Modules:
  0.0 126.4 jit_solution(14680519103823694344)
XLA Ops:
  0.6 1.5 %stack.18 = bf16[1,64,8,4,128]{4,3,2,1,0:T(4,128)(2,1)S(1)} reshape(bf16[64,4096]{1,0:T(8,128)(2,1)} %param.7) | data formatting | bytes 1048576 | tf_op jit(solution)/shard_map/stack | solution.py:146
  2.9 1.1 pad_maximum_fusion
  4.0 7.9 %all-to-all-start = ((bf16[32,2,64,128]{3,2,1,0:T(8,128)(2,1)}), bf16[32,2,64,128]{3,2,1,0:T(8,128)(2,1)S(1)}, u32[]{:S(2)}, u32[]{:S(2)}) async-start(bf16[32,2,64,128]{3,2,1,0:T(8,128)(2,1)} %bitcast.2), calls=%async_computation | async-start | bytes 2097152 | tf_op jit(solution)/shard_map/all_to_all | solution.py:148
  13.5 1.1 pad_maximum_fusion.1
  14.6 14.5 %all-to-all-done.kv = bf16[32,2,64,128]{3,2,1,0:T(8,128)(2,1)S(1)} async-done(((bf16[32,2,64,128]{3,2,1,0:T(8,128)(2,1)}), bf16[32,2,64,128]{3,2,1,0:T(8,128)(2,1)S(1)}, u32[]{:S(2)}, u32[]{:S(2)}) %all-to-all-start) | async-done | bytes 1048608 | tf_op jit(solution)/shard_map/all_to_all | solution.py:148
  29.1 4.0 %all-to-all-start.1 = ((bf16[32,2,64,128]{3,2,1,0:T(8,128)(2,1)}), bf16[32,2,64,128]{3,2,1,0:T(8,128)(2,1)S(1)}, u32[]{:S(2)}, u32[]{:S(2)}) async-start(bf16[32,2,64,128]{3,2,1,0:T(8,128)(2,1)} %bitcast.4), calls=%async_computation.1 | async-start | bytes 2097152 | tf_op jit(solution)/shard_map/all_to_all | solution.py:148
  33.2 2.6 %collective-permute-start = (bf16[24,2,64,128]{3,2,1,0:T(8,128)(2,1)S(1)}, bf16[24,2,64,128]{3,2,1,0:T(8,128)(2,1)S(1)}, u32[]{:S(2)}, u32[]{:S(2)}) collective-permute-start(bf16[24,2,64,128]{3,2,1,0:T(8,128)(2,1)S(1)} %slice.24), channel_id=1, source_target_pairs={{0,32},{32,64},{64,96},{96,128},{128,160},{160,192},{192,224},{224... | collective-permute-start | bytes 2359304 | tf_op jit(solution)/shard_map/ppermute | solution.py:157
  35.8 8.7 %all_gather.3 = s32[4,4,2]{1,2,0:T(2,128)S(1)} all-gather(s32[1,4,2]{1,2,0:T(2,128)S(1)} %copy-done.7), channel_id=1, replica_groups=mesh['z'=16,'y'=4,'h'=8] {'y'}, dimensions={0}, use_global_device_ids=true | all-gather | bytes 160 | tf_op jit(solution)/shard_map/all_gather | solution.py:160
  45.4 0.6 pad.9.docs
  46.0 4.3 %all-to-all-done.1.qd = bf16[32,2,64,128]{3,2,1,0:T(8,128)(2,1)S(1)} async-done(((bf16[32,2,64,128]{3,2,1,0:T(8,128)(2,1)}), bf16[32,2,64,128]{3,2,1,0:T(8,128)(2,1)S(1)}, u32[]{:S(2)}, u32[]{:S(2)}) %all-to-all-start.1) | async-done | bytes 1048608 | tf_op jit(solution)/shard_map/all_to_all | solution.py:148
  50.3 3.5 %collective-permute-done.halo = bf16[24,2,64,128]{3,2,1,0:T(8,128)(2,1)S(1)} collective-permute-done((bf16[24,2,64,128]{3,2,1,0:T(8,128)(2,1)S(1)}, bf16[24,2,64,128]{3,2,1,0:T(8,128)(2,1)S(1)}, u32[]{:S(2)}, u32[]{:S(2)}) %collective-permute-start) | collective-permute-done | bytes 786464 | tf_op jit(solution)/shard_map/ppermute | solution.py:157
  53.8 0.9 copy-done.8
  54.7 17.3 %attend.1 = (bf16[32,2,64,128]{3,2,1,0:T(8,128)(2,1)}, bf16[32,2,64,128]{3,2,1,0:T(8,128)(2,1)}, bf16[24,2,64,128]{3,2,1,0:T(8,128)(2,1)}) custom-call(s32[8]{0:T(128)} %reshape.47.picks, f32[32,128]{1,0:T(8,128)} %pad.9.docs, bf16[32,2,64,128]{3,2,1,0:T(8,128)(2,1)} %copy-done, bf16[24,2,64,128]{3,2,1,0:T(8,128)(2,1)} %copy-done.8, ...), custom_call_target="tpu_custom_call" | custom-call | flops 4831838208 | bytes 6291456 | tf_op jit(solution)/shard_map/attend/pallas_call | solution.py:113
  72.0 3.8 %collective-permute-start.1 = (bf16[24,2,64,128]{3,2,1,0:T(8,128)(2,1)}, bf16[24,2,64,128]{3,2,1,0:T(8,128)(2,1)S(1)}, u32[]{:S(2)}, u32[]{:S(2)}) collective-permute-start(bf16[24,2,64,128]{3,2,1,0:T(8,128)(2,1)} %get-tuple-element.9), channel_id=1, source_target_pairs={{32,0},{64,32},{96,64},{128,96},{160,128},{192,160},{224,192},{256... | collective-permute-start | bytes 2359304 | tf_op jit(solution)/shard_map/ppermute | solution.py:167
  75.9 8.7 %all-to-all-start.2 = ((bf16[32,2,64,128]{3,2,1,0:T(8,128)(2,1)}), bf16[32,2,64,128]{3,2,1,0:T(8,128)(2,1)S(1)}, u32[]{:S(2)}, u32[]{:S(2)}) async-start(bf16[32,2,64,128]{3,2,1,0:T(8,128)(2,1)} %get-tuple-element.7), calls=%async_computation.2 | async-start | bytes 2097152 | tf_op jit(solution)/shard_map/all_to_all | solution.py:151
  84.6 7.4 %collective-permute-done.1 = bf16[24,2,64,128]{3,2,1,0:T(8,128)(2,1)S(1)} collective-permute-done((bf16[24,2,64,128]{3,2,1,0:T(8,128)(2,1)}, bf16[24,2,64,128]{3,2,1,0:T(8,128)(2,1)S(1)}, u32[]{:S(2)}, u32[]{:S(2)}) %collective-permute-start.1) | collective-permute-done | bytes 786464 | tf_op jit(solution)/shard_map/ppermute | solution.py:167
  92.0 1.3 %add_convert_fusion = bf16[32,2,64,128]{3,2,1,0:T(8,128)(2,1)} fusion(bf16[32,2,64,128]{3,2,1,0:T(8,128)(2,1)S(1)} %copy-done.2, bf16[24,2,64,128]{3,2,1,0:T(8,128)(2,1)S(1)} %collective-permute-done.1), kind=kLoop, calls=%fused_computation | loop fusion | flops 2097152 | bytes 2883584 | tf_op jit(solution)/shard_map/convert_element_type | solution.py:170
  93.3 8.5 %all-to-all-done.2 = bf16[32,2,64,128]{3,2,1,0:T(8,128)(2,1)S(1)} async-done(((bf16[32,2,64,128]{3,2,1,0:T(8,128)(2,1)}), bf16[32,2,64,128]{3,2,1,0:T(8,128)(2,1)S(1)}, u32[]{:S(2)}, u32[]{:S(2)}) %all-to-all-start.2) | async-done | bytes 1048608 | tf_op jit(solution)/shard_map/all_to_all | solution.py:151
  101.8 4.0 %all-to-all-start.3 = ((bf16[32,2,64,128]{3,2,1,0:T(8,128)(2,1)}), bf16[32,2,64,128]{3,2,1,0:T(8,128)(2,1)S(1)}, u32[]{:S(2)}, u32[]{:S(2)}) async-start(bf16[32,2,64,128]{3,2,1,0:T(8,128)(2,1)} %add_convert_fusion), calls=%async_computation.3 | async-start | bytes 2097152 | tf_op jit(solution)/shard_map/all_to_all | solution.py:151
  106.3 1.2 squeeze.15
  107.9 1.2 squeeze.14
  109.1 14.0 %all-to-all-done.3 = bf16[32,2,64,128]{3,2,1,0:T(8,128)(2,1)S(1)} async-done(((bf16[32,2,64,128]{3,2,1,0:T(8,128)(2,1)}), bf16[32,2,64,128]{3,2,1,0:T(8,128)(2,1)S(1)}, u32[]{:S(2)}, u32[]{:S(2)}) %all-to-all-start.3) | async-done | bytes 1048608 | tf_op jit(solution)/shard_map/all_to_all | solution.py:151
  123.6 1.2 squeeze.17
  125.2 1.2 squeeze.16
  (34 shorter events, 5.2 us)
Async XLA Ops:
  0.6 1.7 %copy-start.3 = (bf16[64,4096]{1,0:T(8,128)(2,1)S(1)}, bf16[64,4096]{1,0:T(8,128)(2,1)}, u32[]{:S(2)}) copy-start(bf16[64,4096]{1,0:T(8,128)(2,1)} %param.8) | copy-start | bytes 1572868
  4.0 7.9 %copy-start.4 = (bf16[64,4096]{1,0:T(8,128)(2,1)S(1)}, bf16[64,4096]{1,0:T(8,128)(2,1)}, u32[]{:S(2)}) copy-start(bf16[64,4096]{1,0:T(8,128)(2,1)} %param.6) | copy-start | bytes 1572868
  4.0 25.1 %all-to-all-start = ((bf16[32,2,64,128]{3,2,1,0:T(8,128)(2,1)}), bf16[32,2,64,128]{3,2,1,0:T(8,128)(2,1)S(1)}, u32[]{:S(2)}, u32[]{:S(2)}) async-start(bf16[32,2,64,128]{3,2,1,0:T(8,128)(2,1)} %bitcast.2), calls=%async_computation | async-start | bytes 2097152 | tf_op jit(solution)/shard_map/all_to_all | solution.py:148
  11.9 1.0 copy-start.5
  29.1 4.0 %copy-start = (bf16[32,2,64,128]{3,2,1,0:T(8,128)(2,1)}, bf16[32,2,64,128]{3,2,1,0:T(8,128)(2,1)S(1)}, u32[]{:S(2)}) copy-start(bf16[32,2,64,128]{3,2,1,0:T(8,128)(2,1)S(1)} %all-to-all-done.kv) | copy-start | bytes 3145732
  29.1 21.3 %all-to-all-start.1 = ((bf16[32,2,64,128]{3,2,1,0:T(8,128)(2,1)}), bf16[32,2,64,128]{3,2,1,0:T(8,128)(2,1)S(1)}, u32[]{:S(2)}, u32[]{:S(2)}) async-start(bf16[32,2,64,128]{3,2,1,0:T(8,128)(2,1)} %bitcast.4), calls=%async_computation.1 | async-start | bytes 2097152 | tf_op jit(solution)/shard_map/all_to_all | solution.py:148
  33.1 2.8 %copy-start.7 = (s32[1,4,2]{1,2,0:T(2,128)S(1)}, s32[1,4,2]{1,2,0:T(2,128)}, u32[]{:S(2)}) copy-start(s32[1,4,2]{1,2,0:T(2,128)} %param.11) | copy-start | bytes 100
  33.1 12.3 %copy-start.6 = (s32[32768]{0:T(1024)S(1)}, s32[32768]{0:T(1024)}, u32[]{:S(2)}) copy-start(s32[32768]{0:T(1024)} %param.10) | copy-start | bytes 393220
  33.2 20.7 %collective-permute-start = (bf16[24,2,64,128]{3,2,1,0:T(8,128)(2,1)S(1)}, bf16[24,2,64,128]{3,2,1,0:T(8,128)(2,1)S(1)}, u32[]{:S(2)}, u32[]{:S(2)}) collective-permute-start(bf16[24,2,64,128]{3,2,1,0:T(8,128)(2,1)S(1)} %slice.24), channel_id=1, source_target_pairs={{0,32},{32,64},{64,96},{96,128},{128,160},{160,192},{192,224},{224... | collective-permute-start | bytes 2359304 | tf_op jit(solution)/shard_map/ppermute | solution.py:157
  50.3 3.5 %copy-start.1 = (bf16[32,2,64,128]{3,2,1,0:T(8,128)(2,1)}, bf16[32,2,64,128]{3,2,1,0:T(8,128)(2,1)S(1)}, u32[]{:S(2)}) copy-start(bf16[32,2,64,128]{3,2,1,0:T(8,128)(2,1)S(1)} %all-to-all-done.1.qd) | copy-start | bytes 3145732
  53.8 0.9 copy-start.8
  72.0 19.9 %collective-permute-start.1 = (bf16[24,2,64,128]{3,2,1,0:T(8,128)(2,1)}, bf16[24,2,64,128]{3,2,1,0:T(8,128)(2,1)S(1)}, u32[]{:S(2)}, u32[]{:S(2)}) collective-permute-start(bf16[24,2,64,128]{3,2,1,0:T(8,128)(2,1)} %get-tuple-element.9), channel_id=1, source_target_pairs={{32,0},{64,32},{96,64},{128,96},{160,128},{192,160},{224,192},{256... | collective-permute-start | bytes 2359304 | tf_op jit(solution)/shard_map/ppermute | solution.py:167
  75.9 16.1 %copy-start.2 = (bf16[32,2,64,128]{3,2,1,0:T(8,128)(2,1)S(1)}, bf16[32,2,64,128]{3,2,1,0:T(8,128)(2,1)}, u32[]{:S(2)}) copy-start(bf16[32,2,64,128]{3,2,1,0:T(8,128)(2,1)} %get-tuple-element.8) | copy-start | bytes 3145732
  75.9 25.9 %all-to-all-start.2 = ((bf16[32,2,64,128]{3,2,1,0:T(8,128)(2,1)}), bf16[32,2,64,128]{3,2,1,0:T(8,128)(2,1)S(1)}, u32[]{:S(2)}, u32[]{:S(2)}) async-start(bf16[32,2,64,128]{3,2,1,0:T(8,128)(2,1)} %get-tuple-element.7), calls=%async_computation.2 | async-start | bytes 2097152 | tf_op jit(solution)/shard_map/all_to_all | solution.py:151
  101.8 21.3 %all-to-all-start.3 = ((bf16[32,2,64,128]{3,2,1,0:T(8,128)(2,1)}), bf16[32,2,64,128]{3,2,1,0:T(8,128)(2,1)S(1)}, u32[]{:S(2)}, u32[]{:S(2)}) async-start(bf16[32,2,64,128]{3,2,1,0:T(8,128)(2,1)} %add_convert_fusion), calls=%async_computation.3 | async-start | bytes 2097152 | tf_op jit(solution)/shard_map/all_to_all | solution.py:151

commit v2 on v1

v2 whole, which is shorter than its diff:
```python
import math

import jax
import jax.numpy as jnp
from jax import lax
from jax.experimental import pallas as pl
from jax.experimental.pallas import tpu as pltpu
from jax.sharding import Mesh
from jax.sharding import PartitionSpec as P

HEADS = 32
HEAD_DIM = 128
BLOCK = 512
REACH = 3
GROUP = 4
DOCS = 16
CHUNK = 64
PER_BLOCK = BLOCK // CHUNK
NEGATIVE = -1e30
SCALE = HEAD_DIM ** (-0.5)
SCALE_LOG2 = SCALE * math.log2(math.e)
LOW = jnp.bfloat16
MIB = 1024 * 1024

NT = (((1,), (1,)), ((), ()))
NN = (((1,), (0,)), ((), ()))
VMEM = pl.BlockSpec(memory_space=pltpu.VMEM)
SMEM = pl.BlockSpec(memory_space=pltpu.SMEM)
ANY = pl.BlockSpec(memory_space=pl.ANY)


def dot(a, b, dims=NN):
    return lax.dot_general(a, b, dims, preferred_element_type=jnp.float32)


def part_of(ref, block, array):
    start = pl.multiple_of(block * PER_BLOCK, PER_BLOCK)
    rows = ref[pl.ds(start, PER_BLOCK), array * CHUNK : (array + 1) * CHUNK]
    return rows.reshape(BLOCK, HEAD_DIM)


def put_part(ref, block, array, rows):
    start = pl.multiple_of(block * PER_BLOCK, PER_BLOCK)
    rows = rows.astype(LOW).reshape(PER_BLOCK, CHUNK, HEAD_DIM)
    ref[pl.ds(start, PER_BLOCK), array * CHUNK : (array + 1) * CHUNK] = rows


def picks_of(sent, block):
    start = pl.multiple_of(block * PER_BLOCK, PER_BLOCK)
    lines = jnp.max(sent[pl.ds(start, PER_BLOCK)].astype(jnp.float32), axis=0)
    return [jnp.max(lines[i : i + 1]).astype(jnp.int32) for i in range(2)]


def rows_of(block):
    return pl.ds(pl.multiple_of(block * BLOCK, BLOCK), BLOCK)


class Marks:
    def __init__(self, docs):
        self.docs = jnp.transpose(docs[...])
        self.lane = lax.broadcasted_iota(jnp.int32, (128, 128), 1).astype(jnp.float32)

    def same(self, block):
        columns = [self.docs[:, 4 * block + i : 4 * block + i + 1] for i in range(4)]
        return [jnp.broadcast_to(c, (128, 128)) == self.lane for c in columns]

    def keys(self, block):
        return jnp.concatenate([jnp.where(s, 1.0, 0.0).astype(LOW) for s in self.same(block)], axis=0)

    def queries(self, block):
        free = self.lane > DOCS
        parts = [jnp.where(jnp.logical_or(s, free), 0.0, NEGATIVE) for s in self.same(block)]
        return jnp.concatenate(parts, axis=0).astype(LOW)


def causal_mask():
    return lax.broadcasted_iota(jnp.int32, (BLOCK, BLOCK), 0) <= lax.broadcasted_iota(
        jnp.int32, (BLOCK, BLOCK), 1
    )


def score_blocks(keys, slots, query_wide, causal):
    scores = [dot(keys[rows_of(s), :], query_wide, NT) for s in slots]
    scores[-1] = jnp.where(causal, scores[-1], NEGATIVE)
    return scores


def softmax_blocks(scores):
    top = jnp.max(scores[0], axis=0, keepdims=True)
    for s in scores[1:]:
        top = jnp.maximum(top, jnp.max(s, axis=0, keepdims=True))
    top = top * SCALE_LOG2
    probs = [jnp.exp2(s * SCALE_LOG2 - top) for s in scores]
    total = sum(jnp.sum(p, axis=0, keepdims=True) for p in probs)
    return top, total, probs


def finish_block(slots, probs, query, grad, values, keys_t, values_t, add):
    out_t = sum(dot(values_t[s], p) for s, p in zip(slots, probs))
    grad_t = jnp.transpose(grad.astype(jnp.float32))
    delta = jnp.sum(grad_t * out_t, axis=0, keepdims=True)
    query_t = 0.0
    for i, (s, p) in enumerate(zip(slots, probs)):
        prob_grad = dot(values(s), grad, NT)
        score_grad = (p.astype(jnp.float32) * (prob_grad - delta)).astype(LOW)
        query_t = query_t + dot(keys_t[s], score_grad)
        add(i, s, score_grad, p)
    return jnp.transpose(out_t), jnp.transpose(query_t * SCALE)


def last_block(sent, docs, kv, qd, od, part, picks, keys, keys_t, values_t):
    for b in range(GROUP):
        picks[2 * b], picks[2 * b + 1] = picks_of(sent, b)
    marks = Marks(docs)
    for b in range(GROUP):
        key = part_of(kv, b, 0)
        keys[pl.ds(b * BLOCK, BLOCK), :HEAD_DIM] = key
        keys[pl.ds(b * BLOCK, BLOCK), HEAD_DIM:] = marks.keys(REACH + b)
        keys_t[b] = jnp.transpose(key)
        values_t[b] = jnp.transpose(part_of(kv, b, 1))
    own = GROUP - 1
    query, grad = part_of(qd, 0, 0), part_of(qd, 0, 1)
    query_wide = jnp.concatenate([query, marks.queries(REACH + own)], axis=1)
    slots = [own - picks[2 * own], own - picks[2 * own + 1], own]
    scores = score_blocks(keys, slots, query_wide, causal_mask())
    _, total, probs = softmax_blocks(scores)
    inverse = 1.0 / total
    probs = [(p * inverse).astype(LOW) for p in probs]
    unused = own * (own - 1) // 2 - slots[0] - slots[1]
    zero = jnp.zeros((BLOCK, HEAD_DIM), LOW)
    put_part(part, unused, 0, zero)
    put_part(part, unused, 1, zero)

    def add(i, s, score_grad, p):
        put_part(part, s, 0, dot(score_grad, query) * SCALE)
        put_part(part, s, 1, dot(p, grad))

    out, query_grad = finish_block(
        slots, probs, query, grad, lambda s: part_of(kv, s, 1), keys_t, values_t, add
    )
    put_part(od, 0, 0, out)
    put_part(od, 0, 1, query_grad)


def window_slots(picks, j):
    own = REACH + j
    return [own - picks[2 * j], own - picks[2 * j + 1], own]


def totals(picks, docs, kv, key_halo, qd, stats, keys, values_t):
    marks = Marks(docs)
    for b in range(2 * REACH):
        key = part_of(kv, b - REACH, 0) if b >= REACH else key_halo[
            pl.ds(b * PER_BLOCK, PER_BLOCK)
        ].reshape(BLOCK, HEAD_DIM)
        keys[pl.ds(b * BLOCK, BLOCK), :HEAD_DIM] = key
        keys[pl.ds(b * BLOCK, BLOCK), HEAD_DIM:] = marks.keys(b)
    for b in range(REACH):
        values_t[b] = jnp.transpose(part_of(kv, b, 1))
    causal = causal_mask()
    stats[...] = jnp.zeros_like(stats)
    column = lax.broadcasted_iota(jnp.int32, (1, BLOCK), 1)
    line = jnp.zeros((1, BLOCK), jnp.int32)
    for i in range(2 * REACH):
        line = jnp.where(column == i, picks[i], line)
    stats[6:7, :] = line.astype(jnp.float32)
    for j in range(REACH):
        query, grad = part_of(qd, j, 0), part_of(qd, j, 1)
        query_wide = jnp.concatenate([query, marks.queries(REACH + j)], axis=1)
        slots = window_slots(picks, j)
        top, total, probs = softmax_blocks(score_blocks(keys, slots, query_wide, causal))
        stats[j : j + 1, :] = top + jnp.log2(total)
        local_t = dot(values_t[j], probs[-1].astype(LOW))
        if j > 0:
            for s, p in zip(slots[:-1], probs[:-1]):
                here = jnp.where(s >= REACH, 1.0, 0.0)
                local_t += here * dot(values_t[jnp.maximum(s - REACH, 0)], p.astype(LOW))
        grad_t = jnp.transpose(grad.astype(jnp.float32))
        delta = jnp.sum(grad_t * local_t, axis=0, keepdims=True)
        stats[REACH + j : REACH + j + 1, :] = delta / total


def first_blocks(
    picks, docs, kv, key_halo, value_halo, qd, stats, _, od, part,
    keys, values, keys_t, values_t, key_sum, value_sum,
):
    marks = Marks(docs)
    for b in range(2 * REACH):
        rows = pl.ds(b * BLOCK, BLOCK)
        if b < REACH:
            at = pl.ds(b * PER_BLOCK, PER_BLOCK)
            key = key_halo[at].reshape(BLOCK, HEAD_DIM)
            value = value_halo[at].reshape(BLOCK, HEAD_DIM)
        else:
            key, value = part_of(kv, b - REACH, 0), part_of(kv, b - REACH, 1)
        keys[rows, :HEAD_DIM] = key
        keys[rows, HEAD_DIM:] = marks.keys(b)
        values[rows, :] = value
        keys_t[b] = jnp.transpose(key)
        values_t[b] = jnp.transpose(value)
    key_sum[...] = jnp.zeros_like(key_sum)
    value_sum[...] = jnp.zeros_like(value_sum)
    causal = causal_mask()
    for j in range(REACH):
        query, grad = part_of(qd, j, 0), part_of(qd, j, 1)
        query_wide = jnp.concatenate([query, marks.queries(REACH + j)], axis=1)
        slots = window_slots(picks, j)
        log_total = stats[j : j + 1, :]
        scores = score_blocks(keys, slots, query_wide, causal)
        probs = [jnp.exp2(s * SCALE_LOG2 - log_total).astype(LOW) for s in scores]

        def add(i, s, score_grad, p):
            if j == 0 and i < 2:
                return
            key_sum[rows_of(s), :] += dot(score_grad, query)
            value_sum[rows_of(s), :] += dot(p, grad)

        out, query_grad = finish_block(
            slots, probs, query, grad, lambda s: values[rows_of(s), :], keys_t, values_t, add
        )
        put_part(od, j, 0, out)
        put_part(od, j, 1, query_grad)
    for b in range(REACH):
        rows = pl.ds((REACH + b) * BLOCK, BLOCK)
        put_part(part, b, 0, key_sum[rows, :] * SCALE)
        put_part(part, b, 1, value_sum[rows, :])


def later_queries(
    picks, docs, kv, qd_next, stats, last_part, first_part, _, dkv, keys, key_sum, value_sum
):
    marks = Marks(docs)
    for b in range(1, GROUP):
        rows = pl.ds((b - 1) * BLOCK, BLOCK)
        keys[rows, :HEAD_DIM] = part_of(kv, b, 0)
        keys[rows, HEAD_DIM:] = marks.keys(REACH + b)
    key_sum[...] = jnp.zeros_like(key_sum)
    value_sum[...] = jnp.zeros_like(value_sum)
    for j in range(REACH):
        query, grad = part_of(qd_next, j, 0), part_of(qd_next, j, 1)
        query_wide = jnp.concatenate([query, marks.queries(REACH + GROUP + j)], axis=1)
        log_total = stats[j : j + 1, :]
        delta = stats[REACH + j : REACH + j + 1, :]
        first, second = [jnp.maximum(picks[6, 2 * j + i].astype(jnp.int32), 1) for i in range(2)]
        if j == 0:
            chosen = [(GROUP - first, log_total), (GROUP - second, log_total)]
        else:
            chosen = []
            for offset in range(j + 1, REACH + 1):
                used = jnp.logical_or(first == offset, second == offset)
                chosen.append((GROUP + j - offset, jnp.where(used, log_total, -NEGATIVE)))
        probs, products = [], []
        for b, shift in chosen:
            scores = dot(keys[rows_of(b - 1), :], query_wide, NT)
            p = jnp.exp2(scores * SCALE_LOG2 - shift)
            product = p * dot(part_of(kv, b, 1), grad, NT)
            delta = delta + jnp.sum(product, axis=0, keepdims=True)
            probs.append(p)
            products.append(product)
        for (b, _), p, product in zip(chosen, probs, products):
            score_grad = (product - p * delta).astype(LOW)
            key_sum[rows_of(b - 1), :] += dot(score_grad, query)
            value_sum[rows_of(b - 1), :] += dot(p.astype(LOW), grad)
    for b in range(GROUP):
        for array, ref, scale in ((0, key_sum, SCALE), (1, value_sum, 1.0)):
            total = part_of(last_part, b, array).astype(jnp.float32)
            if b < REACH:
                total = total + part_of(first_part, b, array).astype(jnp.float32)
            if b > 0:
                total = total + ref[pl.ds((b - 1) * BLOCK, BLOCK), :] * scale
            put_part(dkv, b, array, total)


def block_spec(shape, index):
    return pl.BlockSpec(shape, lambda *_: index)


def params(mib):
    return pltpu.CompilerParams(vmem_limit_bytes=mib * MIB)


def cost(pairs, products, mib):
    area = pairs * BLOCK * BLOCK
    return pl.CostEstimate(
        flops=2 * products * area * HEAD_DIM, bytes_accessed=mib * MIB, transcendentals=area
    )


def chunks(count, arrays):
    return (count, arrays * CHUNK, HEAD_DIM)


def array(shape, dtype=LOW):
    return jax.ShapeDtypeStruct(shape, dtype)


KV_SPEC = block_spec(chunks(HEADS, 2), (0, 0, 0))
FIRST = REACH * PER_BLOCK


def run_last(docs, x):
    wide, high = 2 * HEAD_DIM, GROUP * BLOCK
    return pl.pallas_call(
        last_block,
        grid=(1,),
        out_shape=(
            array(chunks(HEADS, 4)),
            array(chunks(HEADS, 2)),
            array((2 * GROUP,), jnp.int32),
        ),
        in_specs=[
            block_spec((HEADS, 16, HEAD_DIM), (0, 16, 0)),
            VMEM,
            KV_SPEC,
            block_spec(chunks(PER_BLOCK, 2), (REACH, 1, 0)),
        ],
        out_specs=(block_spec(chunks(PER_BLOCK, 2), (REACH, 0, 0)), KV_SPEC, SMEM),
        scratch_shapes=[
            pltpu.VMEM((high, wide), LOW),
            pltpu.VMEM((GROUP, HEAD_DIM, BLOCK), LOW),
            pltpu.VMEM((GROUP, HEAD_DIM, BLOCK), LOW),
        ],
        compiler_params=params(24),
        cost_estimate=cost(3, 6, 3),
        name="last_block",
    )(x, docs, x, x)


def run_totals(picks, docs, x, key_halo):
    wide, high = 2 * HEAD_DIM, 2 * REACH * BLOCK
    return pl.pallas_call(
        totals,
        grid=(1,),
        out_shape=array((8, BLOCK), jnp.float32),
        in_specs=[
            SMEM,
            VMEM,
            block_spec(chunks(FIRST, 2), (0, 0, 0)),
            VMEM,
            block_spec(chunks(FIRST, 2), (0, 1, 0)),
        ],
        out_specs=VMEM,
        scratch_shapes=[
            pltpu.VMEM((high, wide), LOW),
            pltpu.VMEM((REACH, HEAD_DIM, BLOCK), LOW),
        ],
        compiler_params=params(24),
        cost_estimate=cost(9, 2, 2),
        name="totals",
    )(picks, docs, x, key_halo, x)


def run_first(picks, docs, x, key_halo, value_halo, stats, y):
    wide, high = 2 * HEAD_DIM, 2 * REACH * BLOCK
    return pl.pallas_call(
        first_blocks,
        grid=(1,),
        out_shape=(array(y.shape), array(chunks(FIRST, 2))),
        in_specs=[
            SMEM,
            VMEM,
            block_spec(chunks(FIRST, 2), (0, 0, 0)),
            VMEM,
            VMEM,
            block_spec(chunks(FIRST, 2), (0, 1, 0)),
            VMEM,
            ANY,
        ],
        out_specs=(block_spec(chunks(FIRST, 2), (0, 0, 0)), VMEM),
        scratch_shapes=[
            pltpu.VMEM((high, wide), LOW),
            pltpu.VMEM((high, HEAD_DIM), LOW),
            pltpu.VMEM((2 * REACH, HEAD_DIM, BLOCK), LOW),
            pltpu.VMEM((2 * REACH, HEAD_DIM, BLOCK), LOW),
            pltpu.VMEM((high, HEAD_DIM), jnp.float32),
            pltpu.VMEM((high, HEAD_DIM), jnp.float32),
        ],
        input_output_aliases={7: 0},
        compiler_params=params(32),
        cost_estimate=cost(9, 6, 5),
        name="first_blocks",
    )(picks, docs, x, key_halo, value_halo, x, stats, y)


def run_later(docs, x, qd_next, stats, last_part, first_part, y):
    wide, high = 2 * HEAD_DIM, REACH * BLOCK
    qd_spec = block_spec(chunks(FIRST, 2), (0, 0, 0))
    return pl.pallas_call(
        later_queries,
        grid=(1,),
        out_shape=array(y.shape),
        in_specs=[SMEM, VMEM, KV_SPEC, qd_spec, VMEM, VMEM, VMEM, ANY],
        out_specs=block_spec(chunks(HEADS, 2), (0, 1, 0)),
        scratch_shapes=[
            pltpu.VMEM((high, wide), LOW),
            pltpu.VMEM((high, HEAD_DIM), jnp.float32),
            pltpu.VMEM((high, HEAD_DIM), jnp.float32),
        ],
        input_output_aliases={7: 0},
        compiler_params=params(24),
        cost_estimate=cost(5, 4, 5),
        name="later_queries",
    )(stats, docs, x, qd_next, stats, last_part, first_part, y)


STEPS = 2
STEP_H = PER_BLOCK // STEPS
SENT = 4 * CHUNK + 16


def pack(picks, *args):
    *rows, packed = args
    line = lax.broadcasted_iota(jnp.int32, (16, HEAD_DIM), 0)
    mine = lax.axis_index("h") - pl.program_id(0) * STEP_H
    for k in range(GROUP):
        pair = jnp.where(line == 0, picks[0, 0, k], picks[0, 1, k]).astype(jnp.float32)
        for h in range(STEP_H):
            packed[k, h, 4 * CHUNK :] = jnp.where(mine == h, pair, 0.0).astype(LOW)
            start = (h * GROUP + k) * HEAD_DIM
            for i, ref in enumerate(rows):
                packed[k, h, i * CHUNK : (i + 1) * CHUNK] = ref[:, start : start + HEAD_DIM]


def unpack(packed, *rows):
    for k in range(GROUP):
        for h in range(STEP_H):
            start = (h * GROUP + k) * HEAD_DIM
            for i, ref in enumerate(rows):
                ref[:, start : start + HEAD_DIM] = packed[k, h, i * CHUNK : (i + 1) * CHUNK]


def packed_spec(rows):
    return pl.BlockSpec((GROUP, STEP_H, rows, HEAD_DIM), lambda i: (0, i, 0, 0))


ROWS = pl.BlockSpec((CHUNK, STEP_H * GROUP * HEAD_DIM), lambda i: (0, i))


def run_pack(picks, *rows):
    packed = pl.pallas_call(
        pack,
        grid=(STEPS,),
        out_shape=array((GROUP, PER_BLOCK, SENT, HEAD_DIM)),
        in_specs=[SMEM] + [ROWS] * 4,
        out_specs=packed_spec(SENT),
        cost_estimate=cost(0, 0, 4),
        name="pack",
    )(picks, *rows)
    return packed.reshape(HEADS, SENT, HEAD_DIM)


def run_unpack(packed):
    return pl.pallas_call(
        unpack,
        grid=(STEPS,),
        out_shape=(array((CHUNK, HEADS * HEAD_DIM)),) * 4,
        in_specs=[packed_spec(4 * CHUNK)],
        out_specs=(ROWS,) * 4,
        cost_estimate=cost(0, 0, 4),
        name="unpack",
    )(packed.reshape(GROUP, PER_BLOCK, 4 * CHUNK, HEAD_DIM))


def per_device(queries, key_rows, value_rows, out_grad, doc_ids, picks):
    plane = lax.axis_index("z")
    planes = lax.axis_size("z")
    forward = [(i, i + 1) for i in range(planes - 1)]
    backward = [(i + 1, i) for i in range(planes - 1)]

    def exchange(packed):
        return lax.all_to_all(packed, ("y", "h"), split_axis=0, concat_axis=0)

    x = exchange(run_pack(jnp.swapaxes(picks, 1, 2), key_rows, value_rows, queries, out_grad))

    edge = jnp.full((REACH * BLOCK,), DOCS, jnp.int32)
    docs = jnp.concatenate([edge, doc_ids, edge])
    docs = lax.dynamic_slice_in_dim(
        docs, plane * (GROUP * BLOCK), (2 * REACH + GROUP) * BLOCK, 0
    )
    docs = docs.astype(jnp.float32).reshape(-1, HEAD_DIM)

    key_halo = lax.ppermute(x[PER_BLOCK:, :CHUNK], "z", forward)
    value_halo = lax.ppermute(x[PER_BLOCK:, CHUNK : 2 * CHUNK], "z", forward)
    qd_next = lax.ppermute(x[:FIRST, 2 * CHUNK : 4 * CHUNK], "z", backward)

    y, last_part, picks_here = run_last(docs, x)
    stats = run_totals(picks_here, docs, x, key_halo)
    stats_next = lax.ppermute(stats, "z", backward)
    y, first_part = run_first(picks_here, docs, x, key_halo, value_halo, stats, y)
    y = run_later(docs, x, qd_next, stats_next, last_part, first_part, y)
    return tuple(run_unpack(exchange(y)))


def solution(mesh):
    planes = mesh.shape["seq"] // GROUP
    parts = Mesh(mesh.devices.reshape(planes, GROUP, mesh.shape["head"]), ("z", "y", "h"))
    rows = P(("z", "y", "h"), None)
    return jax.shard_map(
        per_device,
        mesh=parts,
        in_specs=(rows, rows, rows, rows, P(), P(("z", "y"), "h", None)),
        out_specs=(rows,) * 4,
        check_vma=False,
    )
```

time: 127 us -> 116 us (0.913)
  the two profiles are of different devices: /device:TPU:289 before, /device:TPU:257 now
where the time goes in v2:
time: 116 us; the launch traced here: 115 us
  blocking collectives  71.3 us (61%)
  Pallas kernels  28.3 us (24%)
  starting transfers between devices  12.7 us (11%)
  local copies, waits for them, and re-layouts  1.96 us (2%)
    all_to_all x2, blocking collectives, exchange(): return lax.all_to_all(packed, ('y', 'h'), split_axis=0, concat_axis=0)  71.3 us
    pallas_call x1, Pallas kernels, run_first(): pl.pallas_call(first_blocks, grid=(1,), out_shape=(array(y.shape), array(...  8.76 us
    pallas_call x1, Pallas kernels, run_later(): pl.pallas_call(later_queries, grid=(1,), out_shape=array(y.shape), in_spe...  5.49 us
    pallas_call x1, Pallas kernels, run_totals(): pl.pallas_call(totals, grid=(1,), out_shape=array((8, BLOCK), jnp.float32...  4.76 us
    ppermute x1, starting transfers between devices, per_device(): stats_next = lax.ppermute(stats, 'z', backward)  4.33 us
    ppermute x1, starting transfers between devices, per_device(): qd_next = lax.ppermute(x[:FIRST, 2 * CHUNK:4 * CHUNK], 'z', backward)  3.83 us
    pallas_call x1, Pallas kernels, run_last(): pl.pallas_call(last_block, grid=(1,), out_shape=(array(chunks(HEADS, 4)),...  3.67 us
    pallas_call x1, Pallas kernels, run_unpack(): pl.pallas_call(unpack, grid=(STEPS,), out_shape=(array((CHUNK, HEADS * HE...  2.79 us
  transfers between devices with their start and end apart: 4, of which 1 were waited for; matrix products, arithmetic and copies ran while one was open for 1% of the time, Pallas kernels for 15%

profile of v2, /device:TPU:257, one launch (start us, length us, event | category | flops | bytes accessed | tf_op | source)
XLA Modules:
  0.0 115.5 jit_solution(6834635101221757611)
XLA Ops:
  0.6 2.8 %pack.1 = bf16[4,8,272,128]{3,2,1,0:T(8,128)(2,1)} custom-call(s32[1,2,4]{2,1,0:T(2,128)} %bitcast.7, bf16[64,4096]{1,0:T(8,128)(2,1)} %args_0_.4, bf16[64,4096]{1,0:T(8,128)(2,1)} %args_1_.4, bf16[64,4096]{1,0:T(8,128)(2,1)} %args_2_.4, bf16[64,4096]{1,0:T(8,128)(2,1)} %args_3_.4), custom_call_target="tpu_custom_call" | custom-call | bytes 4194304 | tf_op jit(solution)/shard_map/pack/pallas_call | solution.py:440
  3.4 37.9 %all_to_all.10.sent.kv.qd = bf16[32,272,128]{2,1,0:T(8,128)(2,1)S(1)} all-to-all(bf16[32,272,128]{2,1,0:T(8,128)(2,1)} %bitcast.5), channel_id=1, replica_groups=mesh['z'=16,'y'=4,'h'=8] {'y','h'}, dimensions={0} | all-to-all | bytes 4456448 | tf_op jit(solution)/shard_map/all_to_all | solution.py:471
  41.3 0.0 copy-start
  41.3 1.0 fusion.4
  42.3 2.6 %collective-permute-start = (bf16[24,64,128]{2,1,0:T(8,128)(2,1)}, bf16[24,64,128]{2,1,0:T(8,128)(2,1)S(1)}, u32[]{:S(2)}, u32[]{:S(2)}) collective-permute-start(bf16[24,64,128]{2,1,0:T(8,128)(2,1)} %get-tuple-element.15), channel_id=1, source_target_pairs={{0,32},{32,64},{64,96},{96,128},{128,160},{160,192},{192,224},{224... | collective-permute-start | bytes 1179656 | tf_op jit(solution)/shard_map/ppermute | solution.py:482
  44.9 1.0 slice.13
  45.9 3.8 %collective-permute-start.2 = (bf16[24,128,128]{2,1,0:T(8,128)(2,1)}, bf16[24,128,128]{2,1,0:T(8,128)(2,1)S(1)}, u32[]{:S(2)}, u32[]{:S(2)}) collective-permute-start(bf16[24,128,128]{2,1,0:T(8,128)(2,1)} %slice.13), channel_id=1, source_target_pairs={{32,0},{64,32},{96,64},{128,96},{160,128},{192,160},{224,192},{256... | collective-permute-start | bytes 2359304 | tf_op jit(solution)/shard_map/ppermute | solution.py:484
  49.8 1.9 %collective-permute-start.3 = (bf16[24,64,128]{2,1,0:T(8,128)(2,1)}, bf16[24,64,128]{2,1,0:T(8,128)(2,1)}, u32[]{:S(2)}, u32[]{:S(2)}) collective-permute-start(bf16[24,64,128]{2,1,0:T(8,128)(2,1)} %get-tuple-element.14), channel_id=1, source_target_pairs={{0,32},{32,64},{64,96},{96,128},{128,160},{160,192},{192,224},{224... | collective-permute-start | bytes 1179656 | tf_op jit(solution)/shard_map/ppermute | solution.py:483
  51.7 0.0 copy-done
  51.7 0.1 fusion.3.docs
  51.8 3.7 %last_block.1 = (bf16[32,256,128]{2,1,0:T(8,128)(2,1)S(1)}, bf16[32,128,128]{2,1,0:T(8,128)(2,1)S(1)}, s32[8]{0:T(128)S(1)}) custom-call(bf16[32,272,128]{2,1,0:T(8,128)(2,1)S(1)} %all_to_all.10.sent.kv.qd, f32[40,128]{1,0:T(8,128)S(1)} %fusion.3.docs, bf16[32,272,128]{2,1,0:T(8,128)(2,1)S(1)} %all_to_all.10.sent.kv.qd, ...), custom_call_target="tpu_custom_call" | custom-call | flops 1207959552 | bytes 3145728 | tf_op jit(solution)/shard_map/last_block/pallas_call | solution.py:303
  55.5 0.4 collective-permute-done.key_halo
  55.9 4.8 %totals.1.stats = f32[8,512]{1,0:T(8,128)S(1)} custom-call(s32[8]{0:T(128)S(1)} %get-tuple-element.9.picks, f32[40,128]{1,0:T(8,128)S(1)} %fusion.3.docs, bf16[32,272,128]{2,1,0:T(8,128)(2,1)S(1)} %all_to_all.10.sent.kv.qd, bf16[24,64,128]{2,1,0:T(8,128)(2,1)S(1)} %collective-permute-done.key_halo, bf16[32,272,128]{2,1,0:T(8,128)(2,1)S(1)} %all_to_all.10.sent.kv.qd), custom_call_target="tpu_custom_call" | custom-call | flops 1207959552 | bytes 2097152 | tf_op jit(solution)/shard_map/totals/pallas_call | solution.py:331
  60.7 4.3 %collective-permute-start.1 = (f32[8,512]{1,0:T(8,128)S(1)}, f32[8,512]{1,0:T(8,128)S(1)}, u32[]{:S(2)}, u32[]{:S(2)}) collective-permute-start(f32[8,512]{1,0:T(8,128)S(1)} %totals.1.stats), channel_id=1, source_target_pairs={{32,0},{64,32},{96,64},{128,96},{160,128},{192,160},{224,192},{256... | collective-permute-start | bytes 49160 | tf_op jit(solution)/shard_map/ppermute | solution.py:488
  65.0 0.0 collective-permute-done.3.value_halo
  65.0 8.8 %first_blocks.1 = (bf16[32,256,128]{2,1,0:T(8,128)(2,1)S(1)}, bf16[24,128,128]{2,1,0:T(8,128)(2,1)S(1)}) custom-call(s32[8]{0:T(128)S(1)} %get-tuple-element.9.picks, f32[40,128]{1,0:T(8,128)S(1)} %fusion.3.docs, bf16[32,272,128]{2,1,0:T(8,128)(2,1)S(1)} %all_to_all.10.sent.kv.qd, ...), custom_call_target="tpu_custom_call", output_to_operand_aliasing={{0}: (7, {})} | custom-call | flops 3623878656 | bytes 5242880 | tf_op jit(solution)/shard_map/first_blocks/pallas_call | solution.py:355
  73.8 0.0 collective-permute-done.1.picks.stats
  73.8 0.0 collective-permute-done.2.qd_next
  73.8 5.5 %later_queries.1 = bf16[32,256,128]{2,1,0:T(8,128)(2,1)S(1)} custom-call(f32[8,512]{1,0:T(8,128)S(1)} %collective-permute-done.1.picks.stats, f32[40,128]{1,0:T(8,128)S(1)} %fusion.3.docs, bf16[32,272,128]{2,1,0:T(8,128)(2,1)S(1)} %all_to_all.10.sent.kv.qd, bf16[24,128,128]{2,1,0:T(8,128)(2,1)S(1)} %collective-permute-done.2.qd_next, ...), custom_call_target="tpu_custom_call", output_to_operand_aliasing={{}: (7, {})} | custom-call | flops 1342177280 | bytes 5242880 | tf_op jit(solution)/shard_map/later_queries/pallas_call | solution.py:388
  79.3 33.4 %all_to_all.11 = bf16[32,256,128]{2,1,0:T(8,128)(2,1)} all-to-all(bf16[32,256,128]{2,1,0:T(8,128)(2,1)S(1)} %later_queries.1), channel_id=1, replica_groups=mesh['z'=16,'y'=4,'h'=8] {'y','h'}, dimensions={0} | all-to-all | bytes 4194304 | tf_op jit(solution)/shard_map/all_to_all | solution.py:471
  112.7 2.8 %unpack.1 = (bf16[64,4096]{1,0:T(8,128)(2,1)}, bf16[64,4096]{1,0:T(8,128)(2,1)}, bf16[64,4096]{1,0:T(8,128)(2,1)}, bf16[64,4096]{1,0:T(8,128)(2,1)}) custom-call(bf16[4,8,256,128]{3,2,1,0:T(8,128)(2,1)} %bitcast.6), custom_call_target="tpu_custom_call" | custom-call | bytes 4194304 | tf_op jit(solution)/shard_map/unpack/pallas_call | solution.py:453
  (1 shorter events, 0.0 us)
Async XLA Ops:
  41.3 10.4 %copy-start = (s32[32768]{0:T(1024)S(1)}, s32[32768]{0:T(1024)}, u32[]{:S(2)}) copy-start(s32[32768]{0:T(1024)} %param.10) | copy-start | bytes 393220
  42.3 13.6 %collective-permute-start = (bf16[24,64,128]{2,1,0:T(8,128)(2,1)}, bf16[24,64,128]{2,1,0:T(8,128)(2,1)S(1)}, u32[]{:S(2)}, u32[]{:S(2)}) collective-permute-start(bf16[24,64,128]{2,1,0:T(8,128)(2,1)} %get-tuple-element.15), channel_id=1, source_target_pairs={{0,32},{32,64},{64,96},{96,128},{128,160},{160,192},{192,224},{224... | collective-permute-start | bytes 1179656 | tf_op jit(solution)/shard_map/ppermute | solution.py:482
  45.9 27.9 %collective-permute-start.2 = (bf16[24,128,128]{2,1,0:T(8,128)(2,1)}, bf16[24,128,128]{2,1,0:T(8,128)(2,1)S(1)}, u32[]{:S(2)}, u32[]{:S(2)}) collective-permute-start(bf16[24,128,128]{2,1,0:T(8,128)(2,1)} %slice.13), channel_id=1, source_target_pairs={{32,0},{64,32},{96,64},{128,96},{160,128},{192,160},{224,192},{256... | collective-permute-start | bytes 2359304 | tf_op jit(solution)/shard_map/ppermute | solution.py:484
  49.8 15.3 %collective-permute-start.3 = (bf16[24,64,128]{2,1,0:T(8,128)(2,1)}, bf16[24,64,128]{2,1,0:T(8,128)(2,1)}, u32[]{:S(2)}, u32[]{:S(2)}) collective-permute-start(bf16[24,64,128]{2,1,0:T(8,128)(2,1)} %get-tuple-element.14), channel_id=1, source_target_pairs={{0,32},{32,64},{64,96},{96,128},{128,160},{160,192},{192,224},{224... | collective-permute-start | bytes 1179656 | tf_op jit(solution)/shard_map/ppermute | solution.py:483
  60.7 13.1 %collective-permute-start.1 = (f32[8,512]{1,0:T(8,128)S(1)}, f32[8,512]{1,0:T(8,128)S(1)}, u32[]{:S(2)}, u32[]{:S(2)}) collective-permute-start(f32[8,512]{1,0:T(8,128)S(1)} %totals.1.stats), channel_id=1, source_target_pairs={{32,0},{64,32},{96,64},{128,96},{160,128},{192,160},{224,192},{256... | collective-permute-start | bytes 49160 | tf_op jit(solution)/shard_map/ppermute | solution.py:488

commit v3 on v2

v3 whole, which is shorter than its diff:
```python
import math

import jax
import jax.numpy as jnp
from jax import lax
from jax.experimental import pallas as pl
from jax.experimental.pallas import tpu as pltpu
from jax.sharding import Mesh
from jax.sharding import PartitionSpec as P

HEADS = 32
HEAD_DIM = 128
BLOCK = 512
REACH = 3
GROUP = 4
DOCS = 16
CHUNK = 64
PER_BLOCK = BLOCK // CHUNK
NEGATIVE = -1e30
SCALE = HEAD_DIM ** (-0.5)
SCALE_LOG2 = SCALE * math.log2(math.e)
LOW = jnp.bfloat16
MIB = 1024 * 1024

NT = (((1,), (1,)), ((), ()))
NN = (((1,), (0,)), ((), ()))
VMEM = pl.BlockSpec(memory_space=pltpu.VMEM)
SMEM = pl.BlockSpec(memory_space=pltpu.SMEM)


def dot(a, b, dims=NN):
    return lax.dot_general(a, b, dims, preferred_element_type=jnp.float32)


def part_of(ref, block, array):
    start = pl.multiple_of(block * PER_BLOCK, PER_BLOCK)
    rows = ref[pl.ds(start, PER_BLOCK), array * CHUNK : (array + 1) * CHUNK]
    return rows.reshape(BLOCK, HEAD_DIM)


def put_part(ref, block, array, rows):
    start = pl.multiple_of(block * PER_BLOCK, PER_BLOCK)
    rows = rows.astype(LOW).reshape(PER_BLOCK, CHUNK, HEAD_DIM)
    ref[pl.ds(start, PER_BLOCK), array * CHUNK : (array + 1) * CHUNK] = rows


def rows_of(block):
    return pl.ds(pl.multiple_of(block * BLOCK, BLOCK), BLOCK)


class Marks:
    def __init__(self, docs):
        self.rows = docs
        self.docs = jnp.transpose(docs[...])
        self.lane = lax.broadcasted_iota(jnp.int32, (128, 128), 1).astype(jnp.float32)

    def same(self, block):
        columns = [self.docs[:, 4 * block + i : 4 * block + i + 1] for i in range(4)]
        return [jnp.broadcast_to(c, (128, 128)) == self.lane for c in columns]

    def keys(self, block):
        return jnp.concatenate([jnp.where(s, 1.0, 0.0).astype(LOW) for s in self.same(block)], axis=0)

    def wide_t(self, query, block):
        rows = [self.rows[4 * block + i : 4 * block + i + 1, :] for i in range(4)]
        docs = jnp.broadcast_to(jnp.concatenate(rows, axis=1), (HEAD_DIM, BLOCK))
        column = lax.broadcasted_iota(jnp.int32, (HEAD_DIM, BLOCK), 0).astype(jnp.float32)
        free = jnp.logical_or(docs == column, column > DOCS)
        extra = jnp.where(free, 0.0, NEGATIVE).astype(LOW)
        return jnp.concatenate([jnp.transpose(query), extra], axis=0)


def causal_mask():
    return lax.broadcasted_iota(jnp.int32, (BLOCK, BLOCK), 0) <= lax.broadcasted_iota(
        jnp.int32, (BLOCK, BLOCK), 1
    )


def score_blocks(keys, slots, query_wide, causal):
    scores = [dot(keys[rows_of(s), :], query_wide) for s in slots]
    scores[-1] = jnp.where(causal, scores[-1], NEGATIVE)
    return scores


def softmax_blocks(scores):
    top = jnp.max(scores[0], axis=0, keepdims=True)
    for s in scores[1:]:
        top = jnp.maximum(top, jnp.max(s, axis=0, keepdims=True))
    top = top * SCALE_LOG2
    probs = [jnp.exp2(s * SCALE_LOG2 - top) for s in scores]
    total = sum(jnp.sum(p, axis=0, keepdims=True) for p in probs)
    return top, total, probs


def finish_block(slots, probs, query, grad, values, keys_t, values_t, add):
    out_t = sum(dot(values_t[s], p) for s, p in zip(slots, probs))
    grad_t = jnp.transpose(grad)
    delta = jnp.sum(grad_t.astype(jnp.float32) * out_t, axis=0, keepdims=True)
    query_t = 0.0
    for i, (s, p) in enumerate(zip(slots, probs)):
        prob_grad = dot(values(s), grad_t)
        score_grad = (p.astype(jnp.float32) * (prob_grad - delta)).astype(LOW)
        query_t = query_t + dot(keys_t[s], score_grad)
        add(i, s, score_grad, p)
    return jnp.transpose(out_t), jnp.transpose(query_t * SCALE)


def halos(x, key_halo, value_halo, qd_halo):
    key_halo[...] = x[PER_BLOCK:, :CHUNK]
    value_halo[...] = x[PER_BLOCK:, CHUNK : 2 * CHUNK]
    qd_halo[...] = x[:FIRST, 2 * CHUNK : 4 * CHUNK]


def last_block(docs, x, od, part, picks, keys, keys_t, values_t):
    for b in range(GROUP):
        sent = x[b * PER_BLOCK : (b + 1) * PER_BLOCK, 4 * CHUNK :].astype(jnp.float32)
        lines = jnp.max(sent, axis=0)
        for i in range(2):
            picks[2 * b + i] = jnp.max(lines[i : i + 1]).astype(jnp.int32)
    marks = Marks(docs)
    for b in range(GROUP):
        key = part_of(x, b, 0)
        keys[pl.ds(b * BLOCK, BLOCK), :HEAD_DIM] = key
        keys[pl.ds(b * BLOCK, BLOCK), HEAD_DIM:] = marks.keys(REACH + b)
        keys_t[b] = jnp.transpose(key)
        values_t[b] = jnp.transpose(part_of(x, b, 1))
    own = GROUP - 1
    query, grad = part_of(x, own, 2), part_of(x, own, 3)
    query_wide = marks.wide_t(query, REACH + own)
    slots = [own - picks[2 * own], own - picks[2 * own + 1], own]
    scores = score_blocks(keys, slots, query_wide, causal_mask())
    _, total, probs = softmax_blocks(scores)
    inverse = 1.0 / total
    probs = [(p * inverse).astype(LOW) for p in probs]
    unused = own * (own - 1) // 2 - slots[0] - slots[1]
    zero = jnp.zeros((BLOCK, HEAD_DIM), LOW)
    put_part(part, unused, 0, zero)
    put_part(part, unused, 1, zero)

    def add(i, s, score_grad, p):
        put_part(part, s, 0, dot(score_grad, query) * SCALE)
        put_part(part, s, 1, dot(p, grad))

    out, query_grad = finish_block(
        slots, probs, query, grad, lambda s: part_of(x, s, 1), keys_t, values_t, add
    )
    put_part(od, 0, 0, out)
    put_part(od, 0, 1, query_grad)


def window_slots(picks, j):
    own = REACH + j
    return [own - picks[2 * j], own - picks[2 * j + 1], own]


def totals(picks, docs, x, key_halo, stats, probs_out, keys, values_t):
    marks = Marks(docs)
    for b in range(2 * REACH):
        key = part_of(x, b - REACH, 0) if b >= REACH else key_halo[
            pl.ds(b * PER_BLOCK, PER_BLOCK)
        ].reshape(BLOCK, HEAD_DIM)
        keys[pl.ds(b * BLOCK, BLOCK), :HEAD_DIM] = key
        keys[pl.ds(b * BLOCK, BLOCK), HEAD_DIM:] = marks.keys(b)
    for b in range(REACH):
        values_t[b] = jnp.transpose(part_of(x, b, 1))
    causal = causal_mask()
    stats[...] = jnp.zeros_like(stats)
    column = lax.broadcasted_iota(jnp.int32, (1, BLOCK), 1)
    line = jnp.zeros((1, BLOCK), jnp.int32)
    for i in range(2 * REACH):
        line = jnp.where(column == i, picks[i], line)
    stats[6:7, :] = line.astype(jnp.float32)
    def scores_of(j):
        query_wide = marks.wide_t(part_of(x, j, 2), REACH + j)
        slots = window_slots(picks, j)
        return slots, score_blocks(keys, slots, query_wide, causal)

    ahead = scores_of(0)
    for j in range(REACH):
        slots, scores = ahead
        if j + 1 < REACH:
            ahead = scores_of(j + 1)
        top, total, probs = softmax_blocks(scores)
        probs = [p.astype(LOW) for p in probs]
        for i, p in enumerate(probs):
            probs_out[3 * j + i] = p
        stats[j : j + 1, :] = top + jnp.log2(total)
        stats[8 + j : 9 + j, :] = 1.0 / total
        local_t = dot(values_t[j], probs[-1])
        if j > 0:
            for s, p in zip(slots[:-1], probs[:-1]):
                here = jnp.where(s >= REACH, 1.0, 0.0)
                local_t += here * dot(values_t[jnp.maximum(s - REACH, 0)], p)
        grad_t = jnp.transpose(part_of(x, j, 3))
        delta = jnp.sum(grad_t.astype(jnp.float32) * local_t, axis=0, keepdims=True)
        stats[REACH + j : REACH + j + 1, :] = delta / total


def first_blocks(
    picks, x, key_halo, value_halo, stats, probs_in, od, part,
    keys, values, keys_t, values_t, key_sum, value_sum,
):
    for b in range(2 * REACH):
        rows = pl.ds(b * BLOCK, BLOCK)
        if b < REACH:
            at = pl.ds(b * PER_BLOCK, PER_BLOCK)
            key = key_halo[at].reshape(BLOCK, HEAD_DIM)
            value = value_halo[at].reshape(BLOCK, HEAD_DIM)
        else:
            key, value = part_of(x, b - REACH, 0), part_of(x, b - REACH, 1)
        keys[rows, :] = key
        values[rows, :] = value
        keys_t[b] = jnp.transpose(key)
        values_t[b] = jnp.transpose(value)
    key_sum[...] = jnp.zeros_like(key_sum)
    value_sum[...] = jnp.zeros_like(value_sum)
    for j in range(REACH):
        query, grad = part_of(x, j, 2), part_of(x, j, 3)
        slots = window_slots(picks, j)
        inverse = stats[8 + j : 9 + j, :]
        probs = [(probs_in[3 * j + i].astype(jnp.float32) * inverse).astype(LOW) for i in range(3)]

        def add(i, s, score_grad, p):
            if j == 0 and i < 2:
                return
            key_sum[rows_of(s), :] += dot(score_grad, query)
            value_sum[rows_of(s), :] += dot(p, grad)

        out, query_grad = finish_block(
            slots, probs, query, grad, lambda s: values[rows_of(s), :], keys_t, values_t, add
        )
        put_part(od, j, 0, out)
        put_part(od, j, 1, query_grad)
    for b in range(REACH):
        rows = pl.ds((REACH + b) * BLOCK, BLOCK)
        put_part(part, b, 0, key_sum[rows, :] * SCALE)
        put_part(part, b, 1, value_sum[rows, :])


def later_queries(
    picks, docs, x, qd_next, stats, last_od, last_part, first_od, first_part, y,
    keys, key_sum, value_sum,
):
    y[:FIRST, : 2 * CHUNK] = first_od[...]
    y[FIRST:, : 2 * CHUNK] = last_od[...]
    marks = Marks(docs)
    for b in range(1, GROUP):
        rows = pl.ds((b - 1) * BLOCK, BLOCK)
        keys[rows, :HEAD_DIM] = part_of(x, b, 0)
        keys[rows, HEAD_DIM:] = marks.keys(REACH + b)
    key_sum[...] = jnp.zeros_like(key_sum)
    value_sum[...] = jnp.zeros_like(value_sum)
    for j in range(REACH):
        query, grad = part_of(qd_next, j, 0), part_of(qd_next, j, 1)
        query_wide = marks.wide_t(query, REACH + GROUP + j)
        log_total = stats[j : j + 1, :]
        delta = stats[REACH + j : REACH + j + 1, :]
        first, second = [jnp.maximum(picks[6, 2 * j + i].astype(jnp.int32), 1) for i in range(2)]
        if j == 0:
            chosen = [(GROUP - first, log_total), (GROUP - second, log_total)]
        else:
            chosen = []
            for offset in range(j + 1, REACH + 1):
                used = jnp.logical_or(first == offset, second == offset)
                chosen.append((GROUP + j - offset, jnp.where(used, log_total, -NEGATIVE)))
        grad_t = jnp.transpose(grad)
        probs, products = [], []
        for b, shift in chosen:
            scores = dot(keys[rows_of(b - 1), :], query_wide)
            p = jnp.exp2(scores * SCALE_LOG2 - shift)
            product = p * dot(part_of(x, b, 1), grad_t)
            delta = delta + jnp.sum(product, axis=0, keepdims=True)
            probs.append(p)
            products.append(product)
        for (b, _), p, product in zip(chosen, probs, products):
            score_grad = (product - p * delta).astype(LOW)
            key_sum[rows_of(b - 1), :] += dot(score_grad, query)
            value_sum[rows_of(b - 1), :] += dot(p.astype(LOW), grad)
    for b in range(GROUP):
        for array, ref, scale in ((0, key_sum, SCALE), (1, value_sum, 1.0)):
            total = part_of(last_part, b, array).astype(jnp.float32)
            if b < REACH:
                total = total + part_of(first_part, b, array).astype(jnp.float32)
            if b > 0:
                total = total + ref[pl.ds((b - 1) * BLOCK, BLOCK), :] * scale
            put_part(y, b, 2 + array, total)


def params(mib):
    return pltpu.CompilerParams(vmem_limit_bytes=mib * MIB)


def cost(pairs, products, mib):
    area = pairs * BLOCK * BLOCK
    return pl.CostEstimate(
        flops=2 * products * area * HEAD_DIM, bytes_accessed=mib * MIB, transcendentals=area
    )


def chunks(count, arrays):
    return (count, arrays * CHUNK, HEAD_DIM)


def array(shape, dtype=LOW):
    return jax.ShapeDtypeStruct(shape, dtype)


FIRST = REACH * PER_BLOCK


def run_halos(x):
    one, two = array((FIRST, CHUNK, HEAD_DIM)), array(chunks(FIRST, 2))
    return pl.pallas_call(
        halos,
        out_shape=(one, one, two),
        in_specs=[VMEM],
        out_specs=(VMEM,) * 3,
        compiler_params=params(8),
        cost_estimate=cost(0, 0, 3),
        name="halos",
    )(x)


def run_last(docs, x):
    wide, high = 2 * HEAD_DIM, GROUP * BLOCK
    return pl.pallas_call(
        last_block,
        out_shape=(
            array(chunks(PER_BLOCK, 2)),
            array(chunks(HEADS, 2)),
            array((2 * GROUP,), jnp.int32),
        ),
        in_specs=[VMEM, VMEM],
        out_specs=(VMEM, VMEM, SMEM),
        scratch_shapes=[
            pltpu.VMEM((high, wide), LOW),
            pltpu.VMEM((GROUP, HEAD_DIM, BLOCK), LOW),
            pltpu.VMEM((GROUP, HEAD_DIM, BLOCK), LOW),
        ],
        compiler_params=params(24),
        cost_estimate=cost(3, 6, 3),
        name="last_block",
    )(docs, x)


def run_totals(picks, docs, x, key_halo):
    wide, high = 2 * HEAD_DIM, 2 * REACH * BLOCK
    return pl.pallas_call(
        totals,
        out_shape=(array((16, BLOCK), jnp.float32), array((3 * REACH, BLOCK, BLOCK))),
        in_specs=[SMEM, VMEM, VMEM, VMEM],
        out_specs=(VMEM, VMEM),
        scratch_shapes=[
            pltpu.VMEM((high, wide), LOW),
            pltpu.VMEM((REACH, HEAD_DIM, BLOCK), LOW),
        ],
        compiler_params=params(24),
        cost_estimate=cost(9, 2, 2),
        name="totals",
    )(picks, docs, x, key_halo)


def run_first(picks, x, key_halo, value_halo, stats, probs):
    high = 2 * REACH * BLOCK
    return pl.pallas_call(
        first_blocks,
        out_shape=(array(chunks(FIRST, 2)),) * 2,
        in_specs=[SMEM] + [VMEM] * 5,
        out_specs=(VMEM, VMEM),
        scratch_shapes=[
            pltpu.VMEM((high, HEAD_DIM), LOW),
            pltpu.VMEM((high, HEAD_DIM), LOW),
            pltpu.VMEM((2 * REACH, HEAD_DIM, BLOCK), LOW),
            pltpu.VMEM((2 * REACH, HEAD_DIM, BLOCK), LOW),
            pltpu.VMEM((high, HEAD_DIM), jnp.float32),
            pltpu.VMEM((high, HEAD_DIM), jnp.float32),
        ],
        compiler_params=params(32),
        cost_estimate=cost(9, 6, 5),
        name="first_blocks",
    )(picks, x, key_halo, value_halo, stats, probs)


def run_later(docs, x, qd_next, stats, *parts):
    wide, high = 2 * HEAD_DIM, REACH * BLOCK
    return pl.pallas_call(
        later_queries,
        out_shape=array(chunks(HEADS, 4)),
        in_specs=[SMEM] + [VMEM] * 8,
        out_specs=VMEM,
        scratch_shapes=[
            pltpu.VMEM((high, wide), LOW),
            pltpu.VMEM((high, HEAD_DIM), jnp.float32),
            pltpu.VMEM((high, HEAD_DIM), jnp.float32),
        ],
        compiler_params=params(24),
        cost_estimate=cost(5, 4, 5),
        name="later_queries",
    )(stats, docs, x, qd_next, stats, *parts)


SENT = 4 * CHUNK + 16


def pack(picks_sent, k_rows, v_rows, q_rows, d_rows, packed, rows, done, picks, picks_done):
    sources = (k_rows, v_rows, q_rows, d_rows)
    copies = [pltpu.make_async_copy(r, rows.at[i], done.at[i]) for i, r in enumerate(sources)]
    picks_copy = pltpu.make_async_copy(picks_sent, picks, picks_done)
    for copy in copies + [picks_copy]:
        copy.start()
    picks_copy.wait()
    line = lax.broadcasted_iota(jnp.int32, (16, HEAD_DIM), 0)
    mine = lax.axis_index("h")
    for k in range(GROUP):
        pair = jnp.where(line == 0, picks[0, 0, k], picks[0, 1, k]).astype(jnp.float32)
        for h in range(PER_BLOCK):
            packed[k, h, 4 * CHUNK :] = jnp.where(mine == h, pair, 0.0).astype(LOW)
    for i, copy in enumerate(copies):
        copy.wait()
        for k in range(GROUP):
            for h in range(PER_BLOCK):
                start = (h * GROUP + k) * HEAD_DIM
                packed[k, h, i * CHUNK : (i + 1) * CHUNK] = rows[i, :, start : start + HEAD_DIM]


def unpack(packed, out, q_rows, k_rows, v_rows, rows, done):
    copies = []
    for i, target in enumerate((out, q_rows, k_rows, v_rows)):
        for k in range(GROUP):
            for h in range(PER_BLOCK):
                start = (h * GROUP + k) * HEAD_DIM
                rows[i, :, start : start + HEAD_DIM] = packed[k, h, i * CHUNK : (i + 1) * CHUNK]
        copies.append(pltpu.make_async_copy(rows.at[i], target, done.at[i]))
        copies[-1].start()
    for copy in copies:
        copy.wait()


HBM = pl.BlockSpec(memory_space=pltpu.HBM)
STAGING = [pltpu.VMEM((4, CHUNK, HEADS * HEAD_DIM), LOW), pltpu.SemaphoreType.DMA((4,))]


def run_pack(picks, *rows):
    packed = pl.pallas_call(
        pack,
        out_shape=array((GROUP, PER_BLOCK, SENT, HEAD_DIM)),
        in_specs=[HBM] * 5,
        out_specs=VMEM,
        scratch_shapes=STAGING
        + [pltpu.SMEM((1, 2, GROUP), jnp.int32), pltpu.SemaphoreType.DMA],
        compiler_params=params(16),
        cost_estimate=cost(0, 0, 4),
        name="pack",
    )(*[pltpu.with_memory_space_constraint(r, pltpu.HBM) for r in (picks, *rows)])
    return packed.reshape(HEADS, SENT, HEAD_DIM)


def run_unpack(packed):
    return pl.pallas_call(
        unpack,
        out_shape=(array((CHUNK, HEADS * HEAD_DIM)),) * 4,
        in_specs=[VMEM],
        out_specs=(HBM,) * 4,
        scratch_shapes=STAGING,
        compiler_params=params(16),
        cost_estimate=cost(0, 0, 4),
        name="unpack",
    )(packed.reshape(GROUP, PER_BLOCK, 4 * CHUNK, HEAD_DIM))


def per_device(queries, key_rows, value_rows, out_grad, doc_ids, picks):
    plane = lax.axis_index("z")
    planes = lax.axis_size("z")
    forward = [(i, i + 1) for i in range(planes - 1)]
    backward = [(i + 1, i) for i in range(planes - 1)]

    def exchange(packed):
        return lax.all_to_all(packed, ("y", "h"), split_axis=0, concat_axis=0)

    x = exchange(run_pack(jnp.swapaxes(picks, 1, 2), key_rows, value_rows, queries, out_grad))

    edge = jnp.full((REACH * BLOCK,), DOCS, jnp.int32)
    docs = jnp.concatenate([edge, doc_ids, edge])
    docs = lax.dynamic_slice_in_dim(
        docs, plane * (GROUP * BLOCK), (2 * REACH + GROUP) * BLOCK, 0
    )
    docs = docs.astype(jnp.float32).reshape(-1, HEAD_DIM)

    key_halo, value_halo, qd_next = run_halos(x)
    key_halo = lax.ppermute(key_halo, "z", forward)
    value_halo = lax.ppermute(value_halo, "z", forward)
    qd_next = lax.ppermute(qd_next, "z", backward)

    *last, picks_here = run_last(docs, x)
    stats, probs = run_totals(picks_here, docs, x, key_halo)
    stats_next = lax.ppermute(stats[:8], "z", backward)
    first = run_first(picks_here, x, key_halo, value_halo, stats, probs)
    y = run_later(docs, x, qd_next, stats_next, *last, *first)
    return tuple(run_unpack(exchange(y)))


def solution(mesh):
    planes = mesh.shape["seq"] // GROUP
    parts = Mesh(mesh.devices.reshape(planes, GROUP, mesh.shape["head"]), ("z", "y", "h"))
    rows = P(("z", "y", "h"), None)
    return jax.shard_map(
        per_device,
        mesh=parts,
        in_specs=(rows, rows, rows, rows, P(), P(("z", "y"), "h", None)),
        out_specs=(rows,) * 4,
        check_vma=False,
    )
```

time: 116 us -> 110 us (0.948)
  the two profiles are of different devices: /device:TPU:257 before, /device:TPU:385 now
where the time goes in v3:
time: 110 us
  blocking collectives  70.7 us (64%)
  Pallas kernels  24.8 us (23%)
  starting transfers between devices  11.8 us (11%)
  waiting for transfers between devices  1.81 us (2%)
    all_to_all x2, blocking collectives, exchange(): return lax.all_to_all(packed, ('y', 'h'), split_axis=0, concat_axis=0)  70.7 us
    pallas_call x1, Pallas kernels, run_first(): pl.pallas_call(first_blocks, out_shape=(array(chunks(FIRST, 2)),) * 2, in...  6.9 us
    pallas_call x1, Pallas kernels, run_later(): pl.pallas_call(later_queries, out_shape=array(chunks(HEADS, 4)), in_specs...  5.17 us
    pallas_call x1, Pallas kernels, run_totals(): pl.pallas_call(totals, out_shape=(array((16, BLOCK), jnp.float32), array(...  4.65 us
    ppermute x1, starting transfers between devices, per_device(): qd_next = lax.ppermute(qd_next, 'z', backward)  3.85 us
    pallas_call x1, Pallas kernels, run_last(): pl.pallas_call(last_block, out_shape=(array(chunks(PER_BLOCK, 2)), array(...  3.69 us
    ppermute x1, starting transfers between devices, per_device(): stats_next = lax.ppermute(stats[:8], 'z', backward)  3.41 us
    ppermute x1, starting transfers between devices, per_device(): key_halo = lax.ppermute(key_halo, 'z', forward)  2.63 us
  transfers between devices with their start and end apart: 4, of which 2 were waited for; matrix products, arithmetic and copies ran while one was open for 0% of the time, Pallas kernels for 14%

profile of v3, /device:TPU:385, one launch (start us, length us, event | category | flops | bytes accessed | tf_op | source)
XLA Modules:
  0.0 110.1 jit_solution(5854418250368516286)
XLA Ops:
  0.6 1.6 %pack.1 = bf16[4,8,272,128]{3,2,1,0:T(8,128)(2,1)S(1)} custom-call(s32[1,2,4]{2,1,0:T(2,128)} %bitcast.7, bf16[64,4096]{1,0:T(8,128)(2,1)} %k_rows.1, bf16[64,4096]{1,0:T(8,128)(2,1)} %v_rows.1, bf16[64,4096]{1,0:T(8,128)(2,1)} %q_rows.1, bf16[64,4096]{1,0:T(8,128)(2,1)} %d_rows.1), custom_call_target="tpu_custom_call" | custom-call | bytes 4194304 | tf_op jit(solution)/shard_map/pack/pallas_call | solution.py:444
  2.3 37.7 %all_to_all.10.x = bf16[32,272,128]{2,1,0:T(8,128)(2,1)S(1)} all-to-all(bf16[32,272,128]{2,1,0:T(8,128)(2,1)S(1)} %bitcast.5), channel_id=1, replica_groups=mesh['z'=16,'y'=4,'h'=8] {'y','h'}, dimensions={0} | all-to-all | bytes 4456448 | tf_op jit(solution)/shard_map/all_to_all | solution.py:478
  40.0 0.0 copy-start
  40.0 1.2 %halos.1 = (bf16[24,64,128]{2,1,0:T(8,128)(2,1)}, bf16[24,64,128]{2,1,0:T(8,128)(2,1)}, bf16[24,128,128]{2,1,0:T(8,128)(2,1)}) custom-call(bf16[32,272,128]{2,1,0:T(8,128)(2,1)S(1)} %all_to_all.10.x), custom_call_target="tpu_custom_call" | custom-call | bytes 3145728 | tf_op jit(solution)/shard_map/halos/pallas_call | solution.py:313
  41.2 2.6 %collective-permute-start = (bf16[24,64,128]{2,1,0:T(8,128)(2,1)}, bf16[24,64,128]{2,1,0:T(8,128)(2,1)S(1)}, u32[]{:S(2)}, u32[]{:S(2)}) collective-permute-start(bf16[24,64,128]{2,1,0:T(8,128)(2,1)} %get-tuple-element.15), channel_id=1, source_target_pairs={{0,32},{32,64},{64,96},{96,128},{128,160},{160,192},{192,224},{224... | collective-permute-start | bytes 1179656 | tf_op jit(solution)/shard_map/ppermute | solution.py:490
  43.9 3.8 %collective-permute-start.2 = (bf16[24,128,128]{2,1,0:T(8,128)(2,1)}, bf16[24,128,128]{2,1,0:T(8,128)(2,1)S(1)}, u32[]{:S(2)}, u32[]{:S(2)}) collective-permute-start(bf16[24,128,128]{2,1,0:T(8,128)(2,1)} %get-tuple-element.17), channel_id=1, source_target_pairs={{32,0},{64,32},{96,64},{128,96},{160,128},{192,160},{224,192},{256... | collective-permute-start | bytes 2359304 | tf_op jit(solution)/shard_map/ppermute | solution.py:492
  47.7 1.9 %collective-permute-start.3 = (bf16[24,64,128]{2,1,0:T(8,128)(2,1)}, bf16[24,64,128]{2,1,0:T(8,128)(2,1)}, u32[]{:S(2)}, u32[]{:S(2)}) collective-permute-start(bf16[24,64,128]{2,1,0:T(8,128)(2,1)} %get-tuple-element.20), channel_id=1, source_target_pairs={{0,32},{32,64},{64,96},{96,128},{128,160},{160,192},{192,224},{224... | collective-permute-start | bytes 1179656 | tf_op jit(solution)/shard_map/ppermute | solution.py:491
  49.7 0.0 copy-done
  49.7 0.1 fusion.3.docs
  49.8 3.7 %last_block.1 = (bf16[8,128,128]{2,1,0:T(8,128)(2,1)S(1)}, bf16[32,128,128]{2,1,0:T(8,128)(2,1)S(1)}, s32[8]{0:T(128)S(1)}) custom-call(f32[40,128]{1,0:T(8,128)S(1)} %fusion.3.docs, bf16[32,272,128]{2,1,0:T(8,128)(2,1)S(1)} %all_to_all.10.x), custom_call_target="tpu_custom_call" | custom-call | flops 1207959552 | bytes 3145728 | tf_op jit(solution)/shard_map/last_block/pallas_call | solution.py:326
  53.5 1.4 %collective-permute-done.key_halo = bf16[24,64,128]{2,1,0:T(8,128)(2,1)S(1)} collective-permute-done((bf16[24,64,128]{2,1,0:T(8,128)(2,1)}, bf16[24,64,128]{2,1,0:T(8,128)(2,1)S(1)}, u32[]{:S(2)}, u32[]{:S(2)}) %collective-permute-start) | collective-permute-done | bytes 393248 | tf_op jit(solution)/shard_map/ppermute | solution.py:490
  54.9 4.6 %totals.1 = (f32[16,512]{1,0:T(8,128)S(1)}, bf16[9,512,512]{2,1,0:T(8,128)(2,1)S(1)}) custom-call(s32[8]{0:T(128)S(1)} %get-tuple-element.14.picks, f32[40,128]{1,0:T(8,128)S(1)} %fusion.3.docs, bf16[32,272,128]{2,1,0:T(8,128)(2,1)S(1)} %all_to_all.10.x, bf16[24,64,128]{2,1,0:T(8,128)(2,1)S(1)} %collective-permute-done.key_halo), custom_call_target="tpu_custom_call" | custom-call | flops 1207959552 | bytes 2097152 | tf_op jit(solution)/shard_map/totals/pallas_call | solution.py:348
  59.5 3.4 %collective-permute-start.1 = (f32[8,512]{1,0:T(8,128)S(1)}, f32[8,512]{1,0:T(8,128)S(1)}, u32[]{:S(2)}, u32[]{:S(2)}) collective-permute-start(f32[8,512]{1,0:T(8,128)S(1)} %slice.3), channel_id=1, source_target_pairs={{32,0},{64,32},{96,64},{128,96},{160,128},{192,160},{224,192},{256... | collective-permute-start | bytes 49160 | tf_op jit(solution)/shard_map/ppermute | solution.py:496
  62.9 0.5 collective-permute-done.3.value_halo
  63.4 6.9 %first_blocks.1 = (bf16[24,128,128]{2,1,0:T(8,128)(2,1)S(1)}, bf16[24,128,128]{2,1,0:T(8,128)(2,1)S(1)}) custom-call(s32[8]{0:T(128)S(1)} %get-tuple-element.14.picks, bf16[32,272,128]{2,1,0:T(8,128)(2,1)S(1)} %all_to_all.10.x, bf16[24,64,128]{2,1,0:T(8,128)(2,1)S(1)} %collective-permute-done.key_halo, ...), custom_call_target="tpu_custom_call" | custom-call | flops 3623878656 | bytes 5242880 | tf_op jit(solution)/shard_map/first_blocks/pallas_call | solution.py:365
  70.3 0.0 collective-permute-done.1.picks.stats
  70.3 0.0 collective-permute-done.2.qd_next
  70.3 5.2 %later_queries.1 = bf16[32,256,128]{2,1,0:T(8,128)(2,1)S(1)} custom-call(f32[8,512]{1,0:T(8,128)S(1)} %collective-permute-done.1.picks.stats, f32[40,128]{1,0:T(8,128)S(1)} %fusion.3.docs, bf16[32,272,128]{2,1,0:T(8,128)(2,1)S(1)} %all_to_all.10.x, bf16[24,128,128]{2,1,0:T(8,128)(2,1)S(1)} %collective-permute-done.2.qd_next, ...), custom_call_target="tpu_custom_call" | custom-call | flops 1342177280 | bytes 5242880 | tf_op jit(solution)/shard_map/later_queries/pallas_call | solution.py:386
  75.5 33.0 %all_to_all.11 = bf16[32,256,128]{2,1,0:T(8,128)(2,1)S(1)} all-to-all(bf16[32,256,128]{2,1,0:T(8,128)(2,1)S(1)} %later_queries.1), channel_id=1, replica_groups=mesh['z'=16,'y'=4,'h'=8] {'y','h'}, dimensions={0} | all-to-all | bytes 4194304 | tf_op jit(solution)/shard_map/all_to_all | solution.py:478
  108.5 1.4 %unpack.1 = (bf16[64,4096]{1,0:T(8,128)(2,1)}, bf16[64,4096]{1,0:T(8,128)(2,1)}, bf16[64,4096]{1,0:T(8,128)(2,1)}, bf16[64,4096]{1,0:T(8,128)(2,1)}) custom-call(bf16[4,8,256,128]{3,2,1,0:T(8,128)(2,1)S(1)} %bitcast.6), custom_call_target="tpu_custom_call" | custom-call | bytes 4194304 | tf_op jit(solution)/shard_map/unpack/pallas_call | solution.py:459
  (2 shorter events, 0.0 us)
Async XLA Ops:
  40.0 9.7 %copy-start = (s32[32768]{0:T(1024)S(1)}, s32[32768]{0:T(1024)}, u32[]{:S(2)}) copy-start(s32[32768]{0:T(1024)} %param.10) | copy-start | bytes 393220
  41.2 13.6 %collective-permute-start = (bf16[24,64,128]{2,1,0:T(8,128)(2,1)}, bf16[24,64,128]{2,1,0:T(8,128)(2,1)S(1)}, u32[]{:S(2)}, u32[]{:S(2)}) collective-permute-start(bf16[24,64,128]{2,1,0:T(8,128)(2,1)} %get-tuple-element.15), channel_id=1, source_target_pairs={{0,32},{32,64},{64,96},{96,128},{128,160},{160,192},{192,224},{224... | collective-permute-start | bytes 1179656 | tf_op jit(solution)/shard_map/ppermute | solution.py:490
  43.9 26.4 %collective-permute-start.2 = (bf16[24,128,128]{2,1,0:T(8,128)(2,1)}, bf16[24,128,128]{2,1,0:T(8,128)(2,1)S(1)}, u32[]{:S(2)}, u32[]{:S(2)}) collective-permute-start(bf16[24,128,128]{2,1,0:T(8,128)(2,1)} %get-tuple-element.17), channel_id=1, source_target_pairs={{32,0},{64,32},{96,64},{128,96},{160,128},{192,160},{224,192},{256... | collective-permute-start | bytes 2359304 | tf_op jit(solution)/shard_map/ppermute | solution.py:492
  47.7 15.7 %collective-permute-start.3 = (bf16[24,64,128]{2,1,0:T(8,128)(2,1)}, bf16[24,64,128]{2,1,0:T(8,128)(2,1)}, u32[]{:S(2)}, u32[]{:S(2)}) collective-permute-start(bf16[24,64,128]{2,1,0:T(8,128)(2,1)} %get-tuple-element.20), channel_id=1, source_target_pairs={{0,32},{32,64},{64,96},{96,128},{128,160},{160,192},{192,224},{224... | collective-permute-start | bytes 1179656 | tf_op jit(solution)/shard_map/ppermute | solution.py:491
  59.5 10.8 %collective-permute-start.1 = (f32[8,512]{1,0:T(8,128)S(1)}, f32[8,512]{1,0:T(8,128)S(1)}, u32[]{:S(2)}, u32[]{:S(2)}) collective-permute-start(f32[8,512]{1,0:T(8,128)S(1)} %slice.3), channel_id=1, source_target_pairs={{32,0},{64,32},{96,64},{128,96},{160,128},{192,160},{224,192},{256... | collective-permute-start | bytes 49160 | tf_op jit(solution)/shard_map/ppermute | solution.py:496

commit v4 on v3

--- a/solution.py
+++ b/solution.py
@@ -38,10 +38,11 @@
     return rows.reshape(BLOCK, HEAD_DIM)
 
 
-def put_part(ref, block, array, rows):
-    start = pl.multiple_of(block * PER_BLOCK, PER_BLOCK)
-    rows = rows.astype(LOW).reshape(PER_BLOCK, CHUNK, HEAD_DIM)
-    ref[pl.ds(start, PER_BLOCK), array * CHUNK : (array + 1) * CHUNK] = rows
+def put_part(ref, block, array, rows, first=0):
+    start = pl.multiple_of(block * PER_BLOCK, PER_BLOCK) + first // CHUNK
+    count = rows.shape[0] // CHUNK
+    rows = rows.astype(LOW).reshape(count, CHUNK, HEAD_DIM)
+    ref[pl.ds(start, count), array * CHUNK : (array + 1) * CHUNK] = rows
 
 
 def rows_of(block):
@@ -70,38 +71,69 @@
         return jnp.concatenate([jnp.transpose(query), extra], axis=0)
 
 
-def causal_mask():
-    return lax.broadcasted_iota(jnp.int32, (BLOCK, BLOCK), 0) <= lax.broadcasted_iota(
-        jnp.int32, (BLOCK, BLOCK), 1
+HALF = BLOCK // 2
+
+
+def pieces_of(slots):
+    whole = [(s, 0, BLOCK, 0) for s in slots[:-1]]
+    return whole + [(slots[-1], 0, HALF, 0), (slots[-1], HALF, HALF, HALF)]
+
+
+def piece_rows(piece):
+    return pl.ds(pl.multiple_of(piece[0] * BLOCK + piece[1], HALF), piece[2])
+
+
+def plus(total, part, begin):
+    if begin == 0:
+        return total + part
+    return jnp.concatenate([total[:, :begin], total[:, begin:] + part], axis=1)
+
+
+def score_blocks(keys, pieces, query_wide):
+    causal = lax.broadcasted_iota(jnp.int32, (HALF, HALF), 0) <= lax.broadcasted_iota(
+        jnp.int32, (HALF, HALF), 1
     )
-
-
-def score_blocks(keys, slots, query_wide, causal):
-    scores = [dot(keys[rows_of(s), :], query_wide) for s in slots]
-    scores[-1] = jnp.where(causal, scores[-1], NEGATIVE)
-    return scores
-
-
-def softmax_blocks(scores):
+    result = []
+    for piece in pieces:
+        scores = dot(keys[piece_rows(piece), :], query_wide[:, piece[3] :])
+        if piece[2] == HALF:
+            corner = jnp.where(causal, scores[:, :HALF], NEGATIVE)
+            scores = jnp.concatenate([corner, scores[:, HALF:]], axis=1) if piece[3] == 0 else corner
+        result.append(scores)
+    return result
+
+
+def softmax_blocks(pieces, scores):
     top = jnp.max(scores[0], axis=0, keepdims=True)
-    for s in scores[1:]:
-        top = jnp.maximum(top, jnp.max(s, axis=0, keepdims=True))
+    for piece, s in zip(pieces[1:], scores[1:]):
+        begin = piece[3]
+        most = jnp.maximum(top[:, begin:], jnp.max(s, axis=0, keepdims=True))
+        top = most if begin == 0 else jnp.concatenate([top[:, :begin], most], axis=1)
     top = top * SCALE_LOG2
-    probs = [jnp.exp2(s * SCALE_LOG2 - top) for s in scores]
-    total = sum(jnp.sum(p, axis=0, keepdims=True) for p in probs)
+    probs = [jnp.exp2(s * SCALE_LOG2 - top[:, piece[3] :]) for piece, s in zip(pieces, scores)]
+    total = jnp.zeros_like(top)
+    for piece, p in zip(pieces, probs):
+        total = plus(total, jnp.sum(p, axis=0, keepdims=True), piece[3])
     return top, total, probs
 
 
-def finish_block(slots, probs, query, grad, values, keys_t, values_t, add):
-    out_t = sum(dot(values_t[s], p) for s, p in zip(slots, probs))
+def weigh(columns, piece, weights):
+    return dot(columns[piece[0], :, piece[1] : piece[1] + piece[2]], weights)
+
+
+def finish_block(pieces, probs, query, grad, values, keys_t, values_t, add):
+    out_t = jnp.zeros((HEAD_DIM, BLOCK), jnp.float32)
+    for piece, p in zip(pieces, probs):
+        out_t = plus(out_t, weigh(values_t, piece, p), piece[3])
     grad_t = jnp.transpose(grad)
     delta = jnp.sum(grad_t.astype(jnp.float32) * out_t, axis=0, keepdims=True)
-    query_t = 0.0
-    for i, (s, p) in enumerate(zip(slots, probs)):
-        prob_grad = dot(values(s), grad_t)
-        score_grad = (p.astype(jnp.float32) * (prob_grad - delta)).astype(LOW)
-        query_t = query_t + dot(keys_t[s], score_grad)
-        add(i, s, score_grad, p)
+    query_t = jnp.zeros((HEAD_DIM, BLOCK), jnp.float32)
+    for i, (piece, p) in enumerate(zip(pieces, probs)):
+        begin = piece[3]
+        prob_grad = dot(values(piece), grad_t[:, begin:])
+        score_grad = (p.astype(jnp.float32) * (prob_grad - delta[:, begin:])).astype(LOW)
+        query_t = plus(query_t, weigh(keys_t, piece, score_grad), begin)
+        add(i, piece, dot(score_grad, query[begin:]), dot(p, grad[begin:]))
     return jnp.transpose(out_t), jnp.transpose(query_t * SCALE)
 
 
@@ -128,21 +160,26 @@
     query, grad = part_of(x, own, 2), part_of(x, own, 3)
     query_wide = marks.wide_t(query, REACH + own)
     slots = [own - picks[2 * own], own - picks[2 * own + 1], own]
-    scores = score_blocks(keys, slots, query_wide, causal_mask())
-    _, total, probs = softmax_blocks(scores)
+    pieces = pieces_of(slots)
+    _, total, probs = softmax_blocks(pieces, score_blocks(keys, pieces, query_wide))
     inverse = 1.0 / total
-    probs = [(p * inverse).astype(LOW) for p in probs]
+    probs = [(p * inverse[:, piece[3] :]).astype(LOW) for piece, p in zip(pieces, probs)]
     unused = own * (own - 1) // 2 - slots[0] - slots[1]
     zero = jnp.zeros((BLOCK, HEAD_DIM), LOW)
     put_part(part, unused, 0, zero)
     put_part(part, unused, 1, zero)
 
-    def add(i, s, score_grad, p):
-        put_part(part, s, 0, dot(score_grad, query) * SCALE)
-        put_part(part, s, 1, dot(p, grad))
+    def values(piece):
+        first, count = piece[1] // CHUNK, piece[2] // CHUNK
+        at = pl.ds(pl.multiple_of(piece[0] * PER_BLOCK, PER_BLOCK) + first, count)
+        return x[at, CHUNK : 2 * CHUNK].reshape(piece[2], HEAD_DIM)
+
+    def add(i, piece, key_part, value_part):
+        put_part(part, piece[0], 0, key_part * SCALE, piece[1])
+        put_part(part, piece[0], 1, value_part, piece[1])
 
     out, query_grad = finish_block(
-        slots, probs, query, grad, lambda s: part_of(x, s, 1), keys_t, values_t, add
+        pieces, probs, query, grad, values, keys_t, values_t, add
     )
     put_part(od, 0, 0, out)
     put_part(od, 0, 1, query_grad)
@@ -151,6 +188,10 @@
 def window_slots(picks, j):
     own = REACH + j
     return [own - picks[2 * j], own - picks[2 * j + 1], own]
+
+
+def piece_at(j, i, piece):
+    return 3 * j + min(i, 2), pl.ds(piece[1], piece[2]), pl.ds(piece[3], BLOCK - piece[3])
 
 
 def totals(picks, docs, x, key_halo, stats, probs_out, keys, values_t):
@@ -163,7 +204,6 @@
         keys[pl.ds(b * BLOCK, BLOCK), HEAD_DIM:] = marks.keys(b)
     for b in range(REACH):
         values_t[b] = jnp.transpose(part_of(x, b, 1))
-    causal = causal_mask()
     stats[...] = jnp.zeros_like(stats)
     column = lax.broadcasted_iota(jnp.int32, (1, BLOCK), 1)
     line = jnp.zeros((1, BLOCK), jnp.int32)
@@ -173,24 +213,27 @@
     def scores_of(j):
         query_wide = marks.wide_t(part_of(x, j, 2), REACH + j)
         slots = window_slots(picks, j)
-        return slots, score_blocks(keys, slots, query_wide, causal)
+        pieces = pieces_of(slots)
+        return pieces, score_blocks(keys, pieces, query_wide)
 
     ahead = scores_of(0)
     for j in range(REACH):
-        slots, scores = ahead
+        pieces, scores = ahead
         if j + 1 < REACH:
             ahead = scores_of(j + 1)
-        top, total, probs = softmax_blocks(scores)
+        top, total, probs = softmax_blocks(pieces, scores)
         probs = [p.astype(LOW) for p in probs]
-        for i, p in enumerate(probs):
-            probs_out[3 * j + i] = p
         stats[j : j + 1, :] = top + jnp.log2(total)
         stats[8 + j : 9 + j, :] = 1.0 / total
-        local_t = dot(values_t[j], probs[-1])
-        if j > 0:
-            for s, p in zip(slots[:-1], probs[:-1]):
-                here = jnp.where(s >= REACH, 1.0, 0.0)
-                local_t += here * dot(values_t[jnp.maximum(s - REACH, 0)], p)
+        local_t = jnp.zeros((HEAD_DIM, BLOCK), jnp.float32)
+        for i, (piece, p) in enumerate(zip(pieces, probs)):
+            probs_out[piece_at(j, i, piece)] = p
+            if i >= 2:
+                local_t = plus(local_t, weigh(values_t, (j, *piece[1:]), p), piece[3])
+            elif j > 0:
+                here = jnp.where(piece[0] >= REACH, 1.0, 0.0)
+                slot = jnp.maximum(piece[0] - REACH, 0)
+                local_t += here * weigh(values_t, (slot, *piece[1:]), p)
         grad_t = jnp.transpose(part_of(x, j, 3))
         delta = jnp.sum(grad_t.astype(jnp.float32) * local_t, axis=0, keepdims=True)
         stats[REACH + j : REACH + j + 1, :] = delta / total
@@ -198,7 +241,7 @@
 
 def first_blocks(
     picks, x, key_halo, value_halo, stats, probs_in, od, part,
-    keys, values, keys_t, values_t, key_sum, value_sum,
+    values, keys_t, values_t, key_sum, value_sum,
 ):
     for b in range(2 * REACH):
         rows = pl.ds(b * BLOCK, BLOCK)
@@ -208,7 +251,6 @@
             value = value_halo[at].reshape(BLOCK, HEAD_DIM)
         else:
             key, value = part_of(x, b - REACH, 0), part_of(x, b - REACH, 1)
-        keys[rows, :] = key
         values[rows, :] = value
         keys_t[b] = jnp.transpose(key)
         values_t[b] = jnp.transpose(value)
@@ -216,18 +258,22 @@
     value_sum[...] = jnp.zeros_like(value_sum)
     for j in range(REACH):
         query, grad = part_of(x, j, 2), part_of(x, j, 3)
-        slots = window_slots(picks, j)
+        pieces = pieces_of(window_slots(picks, j))
         inverse = stats[8 + j : 9 + j, :]
-        probs = [(probs_in[3 * j + i].astype(jnp.float32) * inverse).astype(LOW) for i in range(3)]
-
-        def add(i, s, score_grad, p):
+        probs = [
+            (probs_in[piece_at(j, i, piece)].astype(jnp.float32) * inverse[:, piece[3] :]).astype(LOW)
+            for i, piece in enumerate(pieces)
+        ]
+
+        def add(i, piece, key_part, value_part):
             if j == 0 and i < 2:
                 return
-            key_sum[rows_of(s), :] += dot(score_grad, query)
-            value_sum[rows_of(s), :] += dot(p, grad)
+            key_sum[piece_rows(piece), :] += key_part
+            value_sum[piece_rows(piece), :] += value_part
 
         out, query_grad = finish_block(
-            slots, probs, query, grad, lambda s: values[rows_of(s), :], keys_t, values_t, add
+            pieces, probs, query, grad, lambda piece: values[piece_rows(piece), :],
+            keys_t, values_t, add,
         )
         put_part(od, j, 0, out)
         put_part(od, j, 1, query_grad)
@@ -238,16 +284,12 @@
 
 
 def later_queries(
-    picks, docs, x, qd_next, stats, last_od, last_part, first_od, first_part, y,
-    keys, key_sum, value_sum,
+    picks, docs, x, qd_next, stats, last_od, last_part, keys, first_od, first_part, y,
+    key_sum, value_sum,
 ):
     y[:FIRST, : 2 * CHUNK] = first_od[...]
     y[FIRST:, : 2 * CHUNK] = last_od[...]
     marks = Marks(docs)
-    for b in range(1, GROUP):
-        rows = pl.ds((b - 1) * BLOCK, BLOCK)
-        keys[rows, :HEAD_DIM] = part_of(x, b, 0)
-        keys[rows, HEAD_DIM:] = marks.keys(REACH + b)
     key_sum[...] = jnp.zeros_like(key_sum)
     value_sum[...] = jnp.zeros_like(value_sum)
     for j in range(REACH):
@@ -266,7 +308,7 @@
         grad_t = jnp.transpose(grad)
         probs, products = [], []
         for b, shift in chosen:
-            scores = dot(keys[rows_of(b - 1), :], query_wide)
+            scores = dot(keys[rows_of(b), :], query_wide)
             p = jnp.exp2(scores * SCALE_LOG2 - shift)
             product = p * dot(part_of(x, b, 1), grad_t)
             delta = delta + jnp.sum(product, axis=0, keepdims=True)
@@ -329,11 +371,11 @@
             array(chunks(PER_BLOCK, 2)),
             array(chunks(HEADS, 2)),
             array((2 * GROUP,), jnp.int32),
+            array((high, wide)),
         ),
         in_specs=[VMEM, VMEM],
-        out_specs=(VMEM, VMEM, SMEM),
+        out_specs=(VMEM, VMEM, SMEM, VMEM),
         scratch_shapes=[
-            pltpu.VMEM((high, wide), LOW),
             pltpu.VMEM((GROUP, HEAD_DIM, BLOCK), LOW),
             pltpu.VMEM((GROUP, HEAD_DIM, BLOCK), LOW),
         ],
@@ -369,7 +411,6 @@
         out_specs=(VMEM, VMEM),
         scratch_shapes=[
             pltpu.VMEM((high, HEAD_DIM), LOW),
-            pltpu.VMEM((high, HEAD_DIM), LOW),
             pltpu.VMEM((2 * REACH, HEAD_DIM, BLOCK), LOW),
             pltpu.VMEM((2 * REACH, HEAD_DIM, BLOCK), LOW),
             pltpu.VMEM((high, HEAD_DIM), jnp.float32),
@@ -382,14 +423,13 @@
 
 
 def run_later(docs, x, qd_next, stats, *parts):
-    wide, high = 2 * HEAD_DIM, REACH * BLOCK
+    high = REACH * BLOCK
     return pl.pallas_call(
         later_queries,
         out_shape=array(chunks(HEADS, 4)),
-        in_specs=[SMEM] + [VMEM] * 8,
+        in_specs=[SMEM] + [VMEM] * 9,
         out_specs=VMEM,
         scratch_shapes=[
-            pltpu.VMEM((high, wide), LOW),
             pltpu.VMEM((high, HEAD_DIM), jnp.float32),
             pltpu.VMEM((high, HEAD_DIM), jnp.float32),
         ],
@@ -491,11 +531,11 @@
     value_halo = lax.ppermute(value_halo, "z", forward)
     qd_next = lax.ppermute(qd_next, "z", backward)
 
-    *last, picks_here = run_last(docs, x)
+    last_od, last_part, picks_here, keys = run_last(docs, x)
     stats, probs = run_totals(picks_here, docs, x, key_halo)
     stats_next = lax.ppermute(stats[:8], "z", backward)
     first = run_first(picks_here, x, key_halo, value_halo, stats, probs)
-    y = run_later(docs, x, qd_next, stats_next, *last, *first)
+    y = run_later(docs, x, qd_next, stats_next, last_od, last_part, keys, *first)
     return tuple(run_unpack(exchange(y)))
 
 

time: 110 us -> 110 us (level)
  the two profiles are of different devices: /device:TPU:385 before, /device:TPU:417 now
where the time goes in v4:
time: 110 us
  blocking collectives  71.7 us (65%)
  Pallas kernels  24.4 us (22%)
  starting transfers between devices  11.9 us (11%)
    all_to_all x2, blocking collectives, exchange(): return lax.all_to_all(packed, ('y', 'h'), split_axis=0, concat_axis=0)  71.7 us
    pallas_call x1, Pallas kernels, run_first(): pl.pallas_call(first_blocks, out_shape=(array(chunks(FIRST, 2)),) * 2, in...  6.57 us
    pallas_call x1, Pallas kernels, run_later(): pl.pallas_call(later_queries, out_shape=array(chunks(HEADS, 4)), in_specs...  4.99 us
    pallas_call x1, Pallas kernels, run_totals(): pl.pallas_call(totals, out_shape=(array((16, BLOCK), jnp.float32), array(...  4.61 us
    ppermute x1, starting transfers between devices, per_device(): stats_next = lax.ppermute(stats[:8], 'z', backward)  4.03 us
    pallas_call x1, Pallas kernels, run_last(): pl.pallas_call(last_block, out_shape=(array(chunks(PER_BLOCK, 2)), array(...  3.87 us
    ppermute x1, starting transfers between devices, per_device(): value_halo = lax.ppermute(value_halo, 'z', forward)  2.65 us
    ppermute x1, starting transfers between devices, per_device(): qd_next = lax.ppermute(qd_next, 'z', backward)  2.64 us
  transfers between devices with their start and end apart: 4, of which 1 were waited for; matrix products, arithmetic and copies ran while one was open for 0% of the time, Pallas kernels for 14%

profile of v4, /device:TPU:417, one launch (start us, length us, event | category | flops | bytes accessed | tf_op | source)
XLA Modules:
  0.0 109.6 jit_solution(14297102394204525115)
XLA Ops:
  0.6 1.6 %pack.1 = bf16[4,8,272,128]{3,2,1,0:T(8,128)(2,1)S(1)} custom-call(s32[1,2,4]{2,1,0:T(2,128)} %bitcast.7, bf16[64,4096]{1,0:T(8,128)(2,1)} %k_rows.1, bf16[64,4096]{1,0:T(8,128)(2,1)} %v_rows.1, bf16[64,4096]{1,0:T(8,128)(2,1)} %q_rows.1, bf16[64,4096]{1,0:T(8,128)(2,1)} %d_rows.1), custom_call_target="tpu_custom_call" | custom-call | bytes 4194304 | tf_op jit(solution)/shard_map/pack/pallas_call | solution.py:484
  2.3 37.7 %all_to_all.10.x = bf16[32,272,128]{2,1,0:T(8,128)(2,1)S(1)} all-to-all(bf16[32,272,128]{2,1,0:T(8,128)(2,1)S(1)} %bitcast.5), channel_id=1, replica_groups=mesh['z'=16,'y'=4,'h'=8] {'y','h'}, dimensions={0} | all-to-all | bytes 4456448 | tf_op jit(solution)/shard_map/all_to_all | solution.py:518
  40.0 0.0 copy-start
  40.0 1.2 %halos.1 = (bf16[24,64,128]{2,1,0:T(8,128)(2,1)}, bf16[24,64,128]{2,1,0:T(8,128)(2,1)}, bf16[24,128,128]{2,1,0:T(8,128)(2,1)}) custom-call(bf16[32,272,128]{2,1,0:T(8,128)(2,1)S(1)} %all_to_all.10.x), custom_call_target="tpu_custom_call" | custom-call | bytes 3145728 | tf_op jit(solution)/shard_map/halos/pallas_call | solution.py:355
  41.2 2.6 %collective-permute-start = (bf16[24,64,128]{2,1,0:T(8,128)(2,1)}, bf16[24,64,128]{2,1,0:T(8,128)(2,1)S(1)}, u32[]{:S(2)}, u32[]{:S(2)}) collective-permute-start(bf16[24,64,128]{2,1,0:T(8,128)(2,1)} %get-tuple-element.16), channel_id=1, source_target_pairs={{0,32},{32,64},{64,96},{96,128},{128,160},{160,192},{192,224},{224... | collective-permute-start | bytes 1179656 | tf_op jit(solution)/shard_map/ppermute | solution.py:530
  43.9 2.6 %collective-permute-start.2 = (bf16[24,128,128]{2,1,0:T(8,128)(2,1)}, bf16[24,128,128]{2,1,0:T(8,128)(2,1)S(1)}, u32[]{:S(2)}, u32[]{:S(2)}) collective-permute-start(bf16[24,128,128]{2,1,0:T(8,128)(2,1)} %get-tuple-element.18), channel_id=1, source_target_pairs={{32,0},{64,32},{96,64},{128,96},{160,128},{192,160},{224,192},{256... | collective-permute-start | bytes 2359304 | tf_op jit(solution)/shard_map/ppermute | solution.py:532
  46.5 2.6 %collective-permute-start.3 = (bf16[24,64,128]{2,1,0:T(8,128)(2,1)}, bf16[24,64,128]{2,1,0:T(8,128)(2,1)}, u32[]{:S(2)}, u32[]{:S(2)}) collective-permute-start(bf16[24,64,128]{2,1,0:T(8,128)(2,1)} %get-tuple-element.22), channel_id=1, source_target_pairs={{0,32},{32,64},{64,96},{96,128},{128,160},{160,192},{192,224},{224... | collective-permute-start | bytes 1179656 | tf_op jit(solution)/shard_map/ppermute | solution.py:531
  49.2 0.0 copy-done
  49.2 0.1 fusion.3.docs
  49.3 3.9 %last_block.1 = (bf16[8,128,128]{2,1,0:T(8,128)(2,1)S(1)}, bf16[32,128,128]{2,1,0:T(8,128)(2,1)S(1)}, s32[8]{0:T(128)S(1)}, bf16[2048,256]{1,0:T(8,128)(2,1)S(1)}) custom-call(f32[40,128]{1,0:T(8,128)S(1)} %fusion.3.docs, bf16[32,272,128]{2,1,0:T(8,128)(2,1)S(1)} %all_to_all.10.x), custom_call_target="tpu_custom_call" | custom-call | flops 1207959552 | bytes 3145728 | tf_op jit(solution)/shard_map/last_block/pallas_call | solution.py:368
  53.2 0.4 collective-permute-done.key_halo
  53.7 4.6 %totals.1 = (f32[16,512]{1,0:T(8,128)S(1)}, bf16[9,512,512]{2,1,0:T(8,128)(2,1)S(1)}) custom-call(s32[8]{0:T(128)S(1)} %get-tuple-element.15.picks, f32[40,128]{1,0:T(8,128)S(1)} %fusion.3.docs, bf16[32,272,128]{2,1,0:T(8,128)(2,1)S(1)} %all_to_all.10.x, bf16[24,64,128]{2,1,0:T(8,128)(2,1)S(1)} %collective-permute-done.key_halo), custom_call_target="tpu_custom_call" | custom-call | flops 1207959552 | bytes 2097152 | tf_op jit(solution)/shard_map/totals/pallas_call | solution.py:390
  58.3 4.0 %collective-permute-start.1 = (f32[8,512]{1,0:T(8,128)S(1)}, f32[8,512]{1,0:T(8,128)S(1)}, u32[]{:S(2)}, u32[]{:S(2)}) collective-permute-start(f32[8,512]{1,0:T(8,128)S(1)} %slice.3), channel_id=1, source_target_pairs={{32,0},{64,32},{96,64},{128,96},{160,128},{192,160},{224,192},{256... | collective-permute-start | bytes 49160 | tf_op jit(solution)/shard_map/ppermute | solution.py:536
  62.3 0.0 collective-permute-done.3.value_halo
  62.3 6.6 %first_blocks.1 = (bf16[24,128,128]{2,1,0:T(8,128)(2,1)S(1)}, bf16[24,128,128]{2,1,0:T(8,128)(2,1)S(1)}) custom-call(s32[8]{0:T(128)S(1)} %get-tuple-element.15.picks, bf16[32,272,128]{2,1,0:T(8,128)(2,1)S(1)} %all_to_all.10.x, bf16[24,64,128]{2,1,0:T(8,128)(2,1)S(1)} %collective-permute-done.key_halo, ...), custom_call_target="tpu_custom_call" | custom-call | flops 3623878656 | bytes 5242880 | tf_op jit(solution)/shard_map/first_blocks/pallas_call | solution.py:407
  68.9 0.0 collective-permute-done.1.picks.stats
  68.9 0.0 collective-permute-done.2.qd_next
  68.9 5.0 %later_queries.1 = bf16[32,256,128]{2,1,0:T(8,128)(2,1)S(1)} custom-call(f32[8,512]{1,0:T(8,128)S(1)} %collective-permute-done.1.picks.stats, f32[40,128]{1,0:T(8,128)S(1)} %fusion.3.docs, bf16[32,272,128]{2,1,0:T(8,128)(2,1)S(1)} %all_to_all.10.x, bf16[24,128,128]{2,1,0:T(8,128)(2,1)S(1)} %collective-permute-done.2.qd_next, ...), custom_call_target="tpu_custom_call" | custom-call | flops 1342177280 | bytes 5242880 | tf_op jit(solution)/shard_map/later_queries/pallas_call | solution.py:427
  73.9 34.0 %all_to_all.11 = bf16[32,256,128]{2,1,0:T(8,128)(2,1)S(1)} all-to-all(bf16[32,256,128]{2,1,0:T(8,128)(2,1)S(1)} %later_queries.1), channel_id=1, replica_groups=mesh['z'=16,'y'=4,'h'=8] {'y','h'}, dimensions={0} | all-to-all | bytes 4194304 | tf_op jit(solution)/shard_map/all_to_all | solution.py:518
  108.0 1.4 %unpack.1 = (bf16[64,4096]{1,0:T(8,128)(2,1)}, bf16[64,4096]{1,0:T(8,128)(2,1)}, bf16[64,4096]{1,0:T(8,128)(2,1)}, bf16[64,4096]{1,0:T(8,128)(2,1)}) custom-call(bf16[4,8,256,128]{3,2,1,0:T(8,128)(2,1)S(1)} %bitcast.6), custom_call_target="tpu_custom_call" | custom-call | bytes 4194304 | tf_op jit(solution)/shard_map/unpack/pallas_call | solution.py:499
  (2 shorter events, 0.0 us)
Async XLA Ops:
  40.0 9.2 %copy-start = (s32[32768]{0:T(1024)S(1)}, s32[32768]{0:T(1024)}, u32[]{:S(2)}) copy-start(s32[32768]{0:T(1024)} %param.10) | copy-start | bytes 393220
  41.2 12.4 %collective-permute-start = (bf16[24,64,128]{2,1,0:T(8,128)(2,1)}, bf16[24,64,128]{2,1,0:T(8,128)(2,1)S(1)}, u32[]{:S(2)}, u32[]{:S(2)}) collective-permute-start(bf16[24,64,128]{2,1,0:T(8,128)(2,1)} %get-tuple-element.16), channel_id=1, source_target_pairs={{0,32},{32,64},{64,96},{96,128},{128,160},{160,192},{192,224},{224... | collective-permute-start | bytes 1179656 | tf_op jit(solution)/shard_map/ppermute | solution.py:530
  43.9 25.0 %collective-permute-start.2 = (bf16[24,128,128]{2,1,0:T(8,128)(2,1)}, bf16[24,128,128]{2,1,0:T(8,128)(2,1)S(1)}, u32[]{:S(2)}, u32[]{:S(2)}) collective-permute-start(bf16[24,128,128]{2,1,0:T(8,128)(2,1)} %get-tuple-element.18), channel_id=1, source_target_pairs={{32,0},{64,32},{96,64},{128,96},{160,128},{192,160},{224,192},{256... | collective-permute-start | bytes 2359304 | tf_op jit(solution)/shard_map/ppermute | solution.py:532
  46.5 15.8 %collective-permute-start.3 = (bf16[24,64,128]{2,1,0:T(8,128)(2,1)}, bf16[24,64,128]{2,1,0:T(8,128)(2,1)}, u32[]{:S(2)}, u32[]{:S(2)}) collective-permute-start(bf16[24,64,128]{2,1,0:T(8,128)(2,1)} %get-tuple-element.22), channel_id=1, source_target_pairs={{0,32},{32,64},{64,96},{96,128},{128,160},{160,192},{192,224},{224... | collective-permute-start | bytes 1179656 | tf_op jit(solution)/shard_map/ppermute | solution.py:531
  58.3 10.6 %collective-permute-start.1 = (f32[8,512]{1,0:T(8,128)S(1)}, f32[8,512]{1,0:T(8,128)S(1)}, u32[]{:S(2)}, u32[]{:S(2)}) collective-permute-start(f32[8,512]{1,0:T(8,128)S(1)} %slice.3), channel_id=1, source_target_pairs={{32,0},{64,32},{96,64},{128,96},{160,128},{192,160},{224,192},{256... | collective-permute-start | bytes 49160 | tf_op jit(solution)/shard_map/ppermute | solution.py:536

commit v5 on v4

--- a/solution.py
+++ b/solution.py
@@ -351,7 +351,7 @@
 
 
 def run_halos(x):
-    one, two = array((FIRST, CHUNK, HEAD_DIM)), array(chunks(FIRST, 2))
+    one, two = pltpu.VMEM((FIRST, CHUNK, HEAD_DIM), LOW), pltpu.VMEM(chunks(FIRST, 2), LOW)
     return pl.pallas_call(
         halos,
         out_shape=(one, one, two),
@@ -379,7 +379,7 @@
             pltpu.VMEM((GROUP, HEAD_DIM, BLOCK), LOW),
             pltpu.VMEM((GROUP, HEAD_DIM, BLOCK), LOW),
         ],
-        compiler_params=params(24),
+        compiler_params=params(16),
         cost_estimate=cost(3, 6, 3),
         name="last_block",
     )(docs, x)
@@ -396,7 +396,7 @@
             pltpu.VMEM((high, wide), LOW),
             pltpu.VMEM((REACH, HEAD_DIM, BLOCK), LOW),
         ],
-        compiler_params=params(24),
+        compiler_params=params(20),
         cost_estimate=cost(9, 2, 2),
         name="totals",
     )(picks, docs, x, key_halo)
@@ -416,10 +416,10 @@
             pltpu.VMEM((high, HEAD_DIM), jnp.float32),
             pltpu.VMEM((high, HEAD_DIM), jnp.float32),
         ],
-        compiler_params=params(32),
+        compiler_params=params(24),
         cost_estimate=cost(9, 6, 5),
         name="first_blocks",
-    )(picks, x, key_halo, value_halo, stats, probs)
+    )(picks, x, key_halo, pltpu.with_memory_space_constraint(value_halo, pltpu.VMEM), stats, probs)
 
 
 def run_later(docs, x, qd_next, stats, *parts):
@@ -433,7 +433,7 @@
             pltpu.VMEM((high, HEAD_DIM), jnp.float32),
             pltpu.VMEM((high, HEAD_DIM), jnp.float32),
         ],
-        compiler_params=params(24),
+        compiler_params=params(16),
         cost_estimate=cost(5, 4, 5),
         name="later_queries",
     )(stats, docs, x, qd_next, stats, *parts)
@@ -488,7 +488,7 @@
         out_specs=VMEM,
         scratch_shapes=STAGING
         + [pltpu.SMEM((1, 2, GROUP), jnp.int32), pltpu.SemaphoreType.DMA],
-        compiler_params=params(16),
+        compiler_params=params(8),
         cost_estimate=cost(0, 0, 4),
         name="pack",
     )(*[pltpu.with_memory_space_constraint(r, pltpu.HBM) for r in (picks, *rows)])
@@ -502,7 +502,7 @@
         in_specs=[VMEM],
         out_specs=(HBM,) * 4,
         scratch_shapes=STAGING,
-        compiler_params=params(16),
+        compiler_params=params(8),
         cost_estimate=cost(0, 0, 4),
         name="unpack",
     )(packed.reshape(GROUP, PER_BLOCK, 4 * CHUNK, HEAD_DIM))

time: 110 us -> 110 us (level)
  no operation moved by 1% of the time
where the time goes in v5:
time: 110 us
  blocking collectives  71.7 us (65%)
  Pallas kernels  24.4 us (22%)
  starting transfers between devices  11.9 us (11%)
    all_to_all x2, blocking collectives, exchange(): return lax.all_to_all(packed, ('y', 'h'), split_axis=0, concat_axis=0)  71.7 us
    pallas_call x1, Pallas kernels, run_first(): pl.pallas_call(first_blocks, out_shape=(array(chunks(FIRST, 2)),) * 2, in...  6.58 us
    pallas_call x1, Pallas kernels, run_later(): pl.pallas_call(later_queries, out_shape=array(chunks(HEADS, 4)), in_specs...  5.03 us
    pallas_call x1, Pallas kernels, run_totals(): pl.pallas_call(totals, out_shape=(array((16, BLOCK), jnp.float32), array(...  4.62 us
    ppermute x1, starting transfers between devices, per_device(): stats_next = lax.ppermute(stats[:8], 'z', backward)  4.02 us
    pallas_call x1, Pallas kernels, run_last(): pl.pallas_call(last_block, out_shape=(array(chunks(PER_BLOCK, 2)), array(...  3.88 us
    ppermute x1, starting transfers between devices, per_device(): value_halo = lax.ppermute(value_halo, 'z', forward)  2.65 us
    ppermute x1, starting transfers between devices, per_device(): qd_next = lax.ppermute(qd_next, 'z', backward)  2.64 us
  transfers between devices with their start and end apart: 4, of which 1 were waited for; matrix products, arithmetic and copies ran while one was open for 0% of the time, Pallas kernels for 14%

profile of v5, /device:TPU:417, one launch (start us, length us, event | category | flops | bytes accessed | tf_op | source)
XLA Modules:
  0.0 109.6 jit_solution(11518220792266792877)
XLA Ops:
  0.6 1.6 %pack.1 = bf16[4,8,272,128]{3,2,1,0:T(8,128)(2,1)S(1)} custom-call(s32[1,2,4]{2,1,0:T(2,128)} %bitcast.7, bf16[64,4096]{1,0:T(8,128)(2,1)} %k_rows.1, bf16[64,4096]{1,0:T(8,128)(2,1)} %v_rows.1, bf16[64,4096]{1,0:T(8,128)(2,1)} %q_rows.1, bf16[64,4096]{1,0:T(8,128)(2,1)} %d_rows.1), custom_call_target="tpu_custom_call" | custom-call | bytes 4194304 | tf_op jit(solution)/shard_map/pack/pallas_call | solution.py:484
  2.3 37.7 %all_to_all.10.x = bf16[32,272,128]{2,1,0:T(8,128)(2,1)S(1)} all-to-all(bf16[32,272,128]{2,1,0:T(8,128)(2,1)S(1)} %bitcast.5), channel_id=1, replica_groups=mesh['z'=16,'y'=4,'h'=8] {'y','h'}, dimensions={0} | all-to-all | bytes 4456448 | tf_op jit(solution)/shard_map/all_to_all | solution.py:518
  40.0 0.0 copy-start
  40.0 1.2 %halos.1 = (bf16[24,64,128]{2,1,0:T(8,128)(2,1)}, bf16[24,64,128]{2,1,0:T(8,128)(2,1)}, bf16[24,128,128]{2,1,0:T(8,128)(2,1)}) custom-call(bf16[32,272,128]{2,1,0:T(8,128)(2,1)S(1)} %all_to_all.10.x), custom_call_target="tpu_custom_call" | custom-call | bytes 3145728 | tf_op jit(solution)/shard_map/halos/pallas_call | solution.py:355
  41.2 2.6 %collective-permute-start = (bf16[24,64,128]{2,1,0:T(8,128)(2,1)}, bf16[24,64,128]{2,1,0:T(8,128)(2,1)S(1)}, u32[]{:S(2)}, u32[]{:S(2)}) collective-permute-start(bf16[24,64,128]{2,1,0:T(8,128)(2,1)} %get-tuple-element.16), channel_id=1, source_target_pairs={{0,32},{32,64},{64,96},{96,128},{128,160},{160,192},{192,224},{224... | collective-permute-start | bytes 1179656 | tf_op jit(solution)/shard_map/ppermute | solution.py:530
  43.9 2.6 %collective-permute-start.2 = (bf16[24,128,128]{2,1,0:T(8,128)(2,1)}, bf16[24,128,128]{2,1,0:T(8,128)(2,1)S(1)}, u32[]{:S(2)}, u32[]{:S(2)}) collective-permute-start(bf16[24,128,128]{2,1,0:T(8,128)(2,1)} %get-tuple-element.18), channel_id=1, source_target_pairs={{32,0},{64,32},{96,64},{128,96},{160,128},{192,160},{224,192},{256... | collective-permute-start | bytes 2359304 | tf_op jit(solution)/shard_map/ppermute | solution.py:532
  46.5 2.6 %collective-permute-start.3 = (bf16[24,64,128]{2,1,0:T(8,128)(2,1)}, bf16[24,64,128]{2,1,0:T(8,128)(2,1)}, u32[]{:S(2)}, u32[]{:S(2)}) collective-permute-start(bf16[24,64,128]{2,1,0:T(8,128)(2,1)} %get-tuple-element.22), channel_id=1, source_target_pairs={{0,32},{32,64},{64,96},{96,128},{128,160},{160,192},{192,224},{224... | collective-permute-start | bytes 1179656 | tf_op jit(solution)/shard_map/ppermute | solution.py:531
  49.2 0.0 copy-done
  49.2 0.1 fusion.3.docs
  49.3 3.9 %last_block.1 = (bf16[8,128,128]{2,1,0:T(8,128)(2,1)S(1)}, bf16[32,128,128]{2,1,0:T(8,128)(2,1)S(1)}, s32[8]{0:T(128)S(1)}, bf16[2048,256]{1,0:T(8,128)(2,1)S(1)}) custom-call(f32[40,128]{1,0:T(8,128)S(1)} %fusion.3.docs, bf16[32,272,128]{2,1,0:T(8,128)(2,1)S(1)} %all_to_all.10.x), custom_call_target="tpu_custom_call" | custom-call | flops 1207959552 | bytes 3145728 | tf_op jit(solution)/shard_map/last_block/pallas_call | solution.py:368
  53.2 0.4 collective-permute-done.key_halo
  53.7 4.6 %totals.1 = (f32[16,512]{1,0:T(8,128)S(1)}, bf16[9,512,512]{2,1,0:T(8,128)(2,1)S(1)}) custom-call(s32[8]{0:T(128)S(1)} %get-tuple-element.15.picks, f32[40,128]{1,0:T(8,128)S(1)} %fusion.3.docs, bf16[32,272,128]{2,1,0:T(8,128)(2,1)S(1)} %all_to_all.10.x, bf16[24,64,128]{2,1,0:T(8,128)(2,1)S(1)} %collective-permute-done.key_halo), custom_call_target="tpu_custom_call" | custom-call | flops 1207959552 | bytes 2097152 | tf_op jit(solution)/shard_map/totals/pallas_call | solution.py:390
  58.3 4.0 %collective-permute-start.1 = (f32[8,512]{1,0:T(8,128)S(1)}, f32[8,512]{1,0:T(8,128)S(1)}, u32[]{:S(2)}, u32[]{:S(2)}) collective-permute-start(f32[8,512]{1,0:T(8,128)S(1)} %slice.3), channel_id=1, source_target_pairs={{32,0},{64,32},{96,64},{128,96},{160,128},{192,160},{224,192},{256... | collective-permute-start | bytes 49160 | tf_op jit(solution)/shard_map/ppermute | solution.py:536
  62.3 0.0 collective-permute-done.3.value_halo
  62.3 6.6 %first_blocks.1 = (bf16[24,128,128]{2,1,0:T(8,128)(2,1)S(1)}, bf16[24,128,128]{2,1,0:T(8,128)(2,1)S(1)}) custom-call(s32[8]{0:T(128)S(1)} %get-tuple-element.15.picks, bf16[32,272,128]{2,1,0:T(8,128)(2,1)S(1)} %all_to_all.10.x, bf16[24,64,128]{2,1,0:T(8,128)(2,1)S(1)} %collective-permute-done.key_halo, ...), custom_call_target="tpu_custom_call" | custom-call | flops 3623878656 | bytes 5242880 | tf_op jit(solution)/shard_map/first_blocks/pallas_call | solution.py:407
  68.9 0.0 collective-permute-done.1.picks.stats
  68.9 0.0 collective-permute-done.2.qd_next
  68.9 5.0 %later_queries.1 = bf16[32,256,128]{2,1,0:T(8,128)(2,1)S(1)} custom-call(f32[8,512]{1,0:T(8,128)S(1)} %collective-permute-done.1.picks.stats, f32[40,128]{1,0:T(8,128)S(1)} %fusion.3.docs, bf16[32,272,128]{2,1,0:T(8,128)(2,1)S(1)} %all_to_all.10.x, bf16[24,128,128]{2,1,0:T(8,128)(2,1)S(1)} %collective-permute-done.2.qd_next, ...), custom_call_target="tpu_custom_call" | custom-call | flops 1342177280 | bytes 5242880 | tf_op jit(solution)/shard_map/later_queries/pallas_call | solution.py:427
  74.0 34.0 %all_to_all.11 = bf16[32,256,128]{2,1,0:T(8,128)(2,1)S(1)} all-to-all(bf16[32,256,128]{2,1,0:T(8,128)(2,1)S(1)} %later_queries.1), channel_id=1, replica_groups=mesh['z'=16,'y'=4,'h'=8] {'y','h'}, dimensions={0} | all-to-all | bytes 4194304 | tf_op jit(solution)/shard_map/all_to_all | solution.py:518
  108.0 1.4 %unpack.1 = (bf16[64,4096]{1,0:T(8,128)(2,1)}, bf16[64,4096]{1,0:T(8,128)(2,1)}, bf16[64,4096]{1,0:T(8,128)(2,1)}, bf16[64,4096]{1,0:T(8,128)(2,1)}) custom-call(bf16[4,8,256,128]{3,2,1,0:T(8,128)(2,1)S(1)} %bitcast.6), custom_call_target="tpu_custom_call" | custom-call | bytes 4194304 | tf_op jit(solution)/shard_map/unpack/pallas_call | solution.py:499
  (2 shorter events, 0.0 us)
Async XLA Ops:
  40.0 9.2 %copy-start = (s32[32768]{0:T(1024)S(1)}, s32[32768]{0:T(1024)}, u32[]{:S(2)}) copy-start(s32[32768]{0:T(1024)} %param.10) | copy-start | bytes 393220
  41.2 12.4 %collective-permute-start = (bf16[24,64,128]{2,1,0:T(8,128)(2,1)}, bf16[24,64,128]{2,1,0:T(8,128)(2,1)S(1)}, u32[]{:S(2)}, u32[]{:S(2)}) collective-permute-start(bf16[24,64,128]{2,1,0:T(8,128)(2,1)} %get-tuple-element.16), channel_id=1, source_target_pairs={{0,32},{32,64},{64,96},{96,128},{128,160},{160,192},{192,224},{224... | collective-permute-start | bytes 1179656 | tf_op jit(solution)/shard_map/ppermute | solution.py:530
  43.9 25.0 %collective-permute-start.2 = (bf16[24,128,128]{2,1,0:T(8,128)(2,1)}, bf16[24,128,128]{2,1,0:T(8,128)(2,1)S(1)}, u32[]{:S(2)}, u32[]{:S(2)}) collective-permute-start(bf16[24,128,128]{2,1,0:T(8,128)(2,1)} %get-tuple-element.18), channel_id=1, source_target_pairs={{32,0},{64,32},{96,64},{128,96},{160,128},{192,160},{224,192},{256... | collective-permute-start | bytes 2359304 | tf_op jit(solution)/shard_map/ppermute | solution.py:532
  46.5 15.8 %collective-permute-start.3 = (bf16[24,64,128]{2,1,0:T(8,128)(2,1)}, bf16[24,64,128]{2,1,0:T(8,128)(2,1)}, u32[]{:S(2)}, u32[]{:S(2)}) collective-permute-start(bf16[24,64,128]{2,1,0:T(8,128)(2,1)} %get-tuple-element.22), channel_id=1, source_target_pairs={{0,32},{32,64},{64,96},{96,128},{128,160},{160,192},{192,224},{224... | collective-permute-start | bytes 1179656 | tf_op jit(solution)/shard_map/ppermute | solution.py:531
  58.3 10.6 %collective-permute-start.1 = (f32[8,512]{1,0:T(8,128)S(1)}, f32[8,512]{1,0:T(8,128)S(1)}, u32[]{:S(2)}, u32[]{:S(2)}) collective-permute-start(f32[8,512]{1,0:T(8,128)S(1)} %slice.3), channel_id=1, source_target_pairs={{32,0},{64,32},{96,64},{128,96},{160,128},{192,160},{224,192},{256... | collective-permute-start | bytes 49160 | tf_op jit(solution)/shard_map/ppermute | solution.py:536
